TPU v7x, 32 devices: a whole 2x2x4 slice. The times are simulated.
32 devices in a mesh: groups: 2 (over x), band: 16 (over z, y, core).
Axes of the slice: x: 2, y: 2, z: 4, core: 2. Of those that a mesh axis runs over, the one named last changes fastest.
Arguments:
- cell_values: bfloat16 [16, 262144], P('groups', 'band'), parts along dimension 0, may hold values from -6 to 6
- slot_block: int32 [16, 16, 3], P('band'), may hold values from 0 to 127
- slot_counts: int32 [16, 16], P('band'), may hold values from 0 to 3, as said below
- slot_tile: int32 [16, 16, 3], P('band'), may hold values from 0 to 255
- remap_tiles: bfloat16 [16, 16, 3, 128, 128], P('band'), may hold values from -0.5 to 0.5
- wave_order: int32 [512], replicated, may hold values from 0 to 511, each once
Outputs:
- spectra: float32 [1024, 2, 8, 512], P(('groups', 'band')), parts along dimension 0
- energy: float32 [8, 512], P('groups', 'band'), parts along dimension 0
There are 2 independent parts, one for each index of `groups`. A program takes and returns all parts, laid end to end along the dimension named above; an argument that names none is the same for every part. Nothing has to cross between parts.
Inputs may be any that keep to these rules, and one draw needn't show every extreme that they name: `slot_counts`: every source device has at least one owner for which all 3 slots are used.
All inputs are finite; a program needn't handle non-finite values.
Results may differ from a plain program's by a relative error of at most 0.0003.
Values may be sent and summed in bfloat16 or wider, within the bound.
A program may use at most 64 MiB of HBM per device.

v0:
```python
import math

import jax
import jax.numpy as jnp
from jax import lax
from jax.sharding import PartitionSpec as P

LATS = 512
LONS = 1024
WAVES = 512
DEG_BLOCK = 128


def gauss_half(lat_count):
    index_vals = jnp.arange(lat_count // 2, dtype=jnp.float32)
    theta = math.pi * (4.0 * index_vals + 3.0) / (4.0 * lat_count + 2.0)
    mu_nodes = (1.0 - (lat_count - 1.0) / (8.0 * float(lat_count) ** 3)) * jnp.cos(theta)
    weights = math.pi / (lat_count + 0.5) * jnp.sqrt(1.0 - mu_nodes * mu_nodes)
    return (mu_nodes, weights)


def dft_tables(wave_vals, lon_count):
    longitude = jnp.arange(lon_count, dtype=jnp.int32)
    phase_int = wave_vals[:, None] * longitude[None, :] % lon_count
    angles = phase_int.astype(jnp.float32) * (2.0 * math.pi / lon_count)
    norm_factor = 1.0 / math.sqrt(lon_count)
    return (jnp.cos(angles) * norm_factor, -jnp.sin(angles) * norm_factor)


def legendre_project(wave_vals, fourier, total_n, deg_block):
    row_count, lat_count, col_count = fourier.shape
    half_lat = lat_count // 2
    mu_nodes, weights = gauss_half(lat_count)
    lat_scale = (weights * math.sqrt(lat_count))[None, :, None]
    north_rows = fourier[:, :half_lat]
    south_rows = fourier[:, half_lat:][:, ::-1]
    even_part = (north_rows + south_rows) * lat_scale
    odd_part = (north_rows - south_rows) * lat_scale
    order_int = wave_vals[:, None]
    order_f = wave_vals.astype(jnp.float32)[:, None]
    sinus = jnp.sqrt(1.0 - mu_nodes * mu_nodes)[None, :]
    start_log = 0.5 * (
        jnp.log(order_f + 0.5)
        + lax.lgamma(order_f + 0.5)
        - lax.lgamma(order_f + 1.0)
        - 0.5 * math.log(math.pi)
    ) + order_f * jnp.log(sinus)
    mu_row = mu_nodes[None, :]

    def inner_step(carried, degree):
        current, previous, log_shift = carried
        degree_f = degree.astype(jnp.float32)
        coef_first = jnp.sqrt(
            jnp.maximum(4.0 * degree_f * degree_f - 1.0, 1.0)
            / jnp.maximum(degree_f * degree_f - order_f * order_f, 1.0)
        )
        coef_second = jnp.sqrt(
            jnp.maximum((degree_f - 1.0) ** 2 - order_f * order_f, 0.0)
            / jnp.maximum(4.0 * (degree_f - 1.0) ** 2 - 1.0, 1.0)
        )
        recurred = coef_first * (mu_row * current - coef_second * previous)
        fresh = jnp.where(
            degree == order_int,
            jnp.ones_like(recurred),
            jnp.where(degree > order_int, recurred, jnp.zeros_like(recurred)),
        )
        too_large = jnp.abs(fresh) > 2.0**50
        factor = jnp.where(too_large, 2.0 ** (-50), 1.0)
        fresh = fresh * factor
        moved = current * factor
        log_shift = log_shift + jnp.where(too_large, 50.0 * math.log(2.0), 0.0)
        legendre = fresh * jnp.exp(start_log + log_shift)
        return ((fresh, moved, log_shift), legendre)

    def outer_step(carried, block_start):
        degrees = block_start + jnp.arange(deg_block, dtype=jnp.int32)
        carried, legendre_block = lax.scan(inner_step, carried, degrees, unroll=8)
        even_out = jnp.einsum(
            "nrl,rlc->rnc", legendre_block, even_part, precision=lax.Precision.HIGHEST
        )
        odd_out = jnp.einsum(
            "nrl,rlc->rnc", legendre_block, odd_part, precision=lax.Precision.HIGHEST
        )
        parity = ((degrees[None, :] - order_int) % 2 == 0)[:, :, None]
        return (carried, jnp.where(parity, even_out, odd_out))

    zero_state = jnp.zeros((row_count, half_lat), jnp.float32)
    starts = jnp.arange(0, total_n, deg_block, dtype=jnp.int32)
    _, blocked = lax.scan(outer_step, (zero_state, zero_state, zero_state), starts)
    return blocked.transpose(1, 3, 0, 2).reshape(row_count, col_count, total_n)


def energy_terms(wave_vals, spectra, levels):
    row_count = spectra.shape[0]
    total_n = spectra.shape[2]
    squares = (spectra * spectra).reshape(row_count, 2, 2, levels, total_n)
    summed = jnp.sum(squares, axis=(1, 2))
    weights = jnp.where(wave_vals == 0, 1.0, 2.0).astype(jnp.float32)
    degree_f = jnp.arange(total_n, dtype=jnp.float32)
    return (
        jnp.sum(summed * weights[:, None, None], axis=0) / (2.0 * (2.0 * degree_f + 1.0))[None, :]
    )


def shards(cell_values, slot_block, slot_counts, slot_tile, remap_tiles, wave_order):
    peer_count = lax.axis_size("band")
    band_index = lax.axis_index("band")
    field_rows, cell_dev = cell_values.shape
    capacity = slot_block.shape[2]
    block_cells = remap_tiles.shape[3]
    tile_width = remap_tiles.shape[4]
    lat_dev = LATS // peer_count
    tile_dev = lat_dev * (LONS // tile_width)
    wave_dev = WAVES // peer_count
    blocks = cell_values.reshape(field_rows, cell_dev // block_cells, block_cells).transpose(
        1, 0, 2
    )
    picked = blocks[slot_block[0]]
    is_valid = jnp.arange(capacity, dtype=jnp.int32)[None, :] < slot_counts[0][:, None]
    picked = jnp.where(is_valid[:, :, None, None], picked, jnp.zeros_like(picked))
    arrived = lax.all_to_all(picked, "band", split_axis=0, concat_axis=0, tiled=True)
    contribs = jnp.einsum(
        "skfc,skcg->skfg", arrived, remap_tiles[0], preferred_element_type=jnp.float32
    )
    tile_ids = slot_tile[0].reshape(-1)
    onehot = (jnp.arange(tile_dev, dtype=jnp.int32)[:, None] == tile_ids[None, :]).astype(
        jnp.float32
    )
    assembled = jnp.dot(
        onehot,
        contribs.reshape(-1, field_rows * tile_width),
        precision=lax.Precision.HIGHEST,
        preferred_element_type=jnp.float32,
    )
    lat_field = (
        assembled.reshape(lat_dev, LONS // tile_width, field_rows, tile_width)
        .transpose(0, 2, 1, 3)
        .reshape(lat_dev * field_rows, LONS)
    )
    cosine, sine_table = dft_tables(wave_order, LONS)
    dims = (((1,), (1,)), ((), ()))
    real_part = lax.dot_general(
        cosine, lat_field, dims, precision=lax.Precision.HIGHEST, preferred_element_type=jnp.float32
    )
    imag_part = lax.dot_general(
        sine_table,
        lat_field,
        dims,
        precision=lax.Precision.HIGHEST,
        preferred_element_type=jnp.float32,
    )
    fourier = jnp.stack(
        [
            real_part.reshape(WAVES, lat_dev, field_rows),
            imag_part.reshape(WAVES, lat_dev, field_rows),
        ],
        axis=2,
    ).reshape(WAVES, lat_dev * 2 * field_rows)
    regrouped = lax.all_to_all(fourier, "band", split_axis=0, concat_axis=1, tiled=True)
    local_waves = lax.dynamic_slice_in_dim(wave_order, band_index * wave_dev, wave_dev, 0)
    spectra = legendre_project(
        local_waves, regrouped.reshape(wave_dev, LATS, 2 * field_rows), WAVES, DEG_BLOCK
    )
    partial_value = energy_terms(local_waves, spectra, field_rows // 2)
    energy = lax.psum_scatter(partial_value, "band", scatter_dimension=1, tiled=True)
    return (spectra.reshape(wave_dev, 2, field_rows, WAVES), energy)


def solution(mesh):
    in_specs = (
        P("groups", "band"),
        P("band", None, None),
        P("band", None),
        P("band", None, None),
        P("band", None, None, None, None),
        P(),
    )
    out_specs = (P(("groups", "band"), None, None, None), P("groups", "band"))
    return jax.shard_map(shards, mesh=mesh, in_specs=in_specs, out_specs=out_specs, check_vma=False)
```

profile of v0, /device:TPU:0, one launch (start us, length us, event | category | flops | bytes accessed | tf_op | source)
XLA Modules:
  0.0 1075.9 jit_solution(4046338397227477579)
XLA Ops:
  11.2 7.4 all-to-all-start
  19.5 6.5 all-to-all-done
  28.3 11.3 %fusion.71 = f32[512,32,1,8]{0,1,3,2:T(8,128)S(1)} fusion(s32[512]{0:T(512)S(1)} %copy-done.5, f32[32,8,1024]{2,1,0:T(8,128)} %reshape.788), kind=kOutput, calls=%fused_computation.154 | convolution fusion | flops 1618477056 | bytes 1574912 | tf_op jit(solution)/shard_map/dot_general | solution.py:142
  39.6 10.3 fusion.74
  60.8 22.5 %all-to-all-done.1 = f32[16,32,512]{2,1,0:T(8,128)S(1)} async-done(((f32[16,32,512]{2,1,0:T(8,128)}), f32[16,32,512]{2,1,0:T(8,128)S(1)}, u32[]{:S(2)}, u32[]{:S(2)}) %all-to-all-start.1) | async-done | bytes 1048608 | tf_op jit(solution)/shard_map/all_to_all | solution.py:159
  83.3 11.7 %copy.37 = f32[32,16,512]{0,2,1:T(8,128)} copy(f32[32,16,512]{2,0,1:T(8,128)S(1)} %bitcast.234) | data formatting | bytes 2097152 | tf_op jit(solution)/shard_map/all_to_all | solution.py:159
  105.6 896.2 %while.58 = (s32[]{:T(128)}, f32[32,256]{1,0:T(8,128)S(1)}, f32[32,256]{1,0:T(8,128)S(1)}, f32[32,256]{1,0:T(8,128)S(1)}, f32[4,32,128,16]{2,3,1,0:T(8,128)}, /*...) while((s32[]{:T(128)}, f32[32,256]{1,0:T(8,128)S(1)}, ...), condition=%wide.region_3.4_spmd.clone.clone, body=%wide.region_0.3_spmd.clone.clone.sunk | while | flops 405102176 | bytes 29388604 | solution.py:89
  107.0 206.9 %while.59 = (s32[]{:T(128)}, f32[32,256]{1,0:T(8,128)S(1)}, f32[32,256]{1,0:T(8,128)S(1)}, f32[32,256]{1,0:T(8,128)S(1)}, f32[16,8,32,256]{3,2,1,0:T(8,128)}, /*...) while((s32[]{:T(128)}, f32[32,256]{1,0:T(8,128)S(1)}, ...), condition=%wide.region_2.2_spmd.clone, body=%wide.region_1.1_spmd.clone.sunk | while | flops 2312281 | bytes 2341993 | solution.py:77
  113.0 5.1 compare_bitcast_fusion.17
  125.9 5.1 compare_bitcast_fusion.17
  138.8 5.1 compare_bitcast_fusion.17
  151.8 5.1 compare_bitcast_fusion.17
  313.9 8.2 fusion.124
  322.9 6.7 fusion.126
  331.0 206.9 %while.59 = (s32[]{:T(128)}, f32[32,256]{1,0:T(8,128)S(1)}, f32[32,256]{1,0:T(8,128)S(1)}, f32[32,256]{1,0:T(8,128)S(1)}, f32[16,8,32,256]{3,2,1,0:T(8,128)}, /*...) while((s32[]{:T(128)}, f32[32,256]{1,0:T(8,128)S(1)}, ...), condition=%wide.region_2.2_spmd.clone, body=%wide.region_1.1_spmd.clone.sunk | while | flops 2312281 | bytes 2341993 | solution.py:77
  537.9 8.2 fusion.124
  546.9 6.7 fusion.126
  555.0 206.9 %while.59 = (s32[]{:T(128)}, f32[32,256]{1,0:T(8,128)S(1)}, f32[32,256]{1,0:T(8,128)S(1)}, f32[32,256]{1,0:T(8,128)S(1)}, f32[16,8,32,256]{3,2,1,0:T(8,128)}, /*...) while((s32[]{:T(128)}, f32[32,256]{1,0:T(8,128)S(1)}, ...), condition=%wide.region_2.2_spmd.clone, body=%wide.region_1.1_spmd.clone.sunk | while | flops 2312281 | bytes 2341993 | solution.py:77
  761.9 8.2 fusion.124
  770.9 6.7 fusion.126
  779.0 206.9 %while.59 = (s32[]{:T(128)}, f32[32,256]{1,0:T(8,128)S(1)}, f32[32,256]{1,0:T(8,128)S(1)}, f32[32,256]{1,0:T(8,128)S(1)}, f32[16,8,32,256]{3,2,1,0:T(8,128)}, /*...) while((s32[]{:T(128)}, f32[32,256]{1,0:T(8,128)S(1)}, ...), condition=%wide.region_2.2_spmd.clone, body=%wide.region_1.1_spmd.clone.sunk | while | flops 2312281 | bytes 2341993 | solution.py:77
  985.9 8.2 fusion.124
  994.9 6.7 fusion.126
  1014.1 53.3 %reduce-scatter.4.cloned.1.call-done = f32[32,4]{1,0:T(8,128)} async-done(((f32[512,4]{1,0:T(8,128)}), f32[32,4]{1,0:T(8,128)}) %reduce-scatter.4.cloned.1.call-update) | async-done | bytes 528
  (1047 shorter events, 517.0 us)
Async XLA Ops:
  7.2 18.9 %copy-start = (bf16[1,16,3,128,128]{4,3,2,1,0:T(8,128)(2,1)S(1)}, bf16[1,16,3,128,128]{4,3,2,1,0:T(8,128)(2,1)}, u32[]{:S(2)}) copy-start(bf16[1,16,3,128,128]{4,3,2,1,0:T(8,128)(2,1)} %param.14) | copy-start | bytes 4718596
  11.2 14.8 %all-to-all-start = ((bf16[16,3,8,128]{3,2,1,0:T(8,128)(2,1)}), bf16[16,3,8,128]{3,2,1,0:T(8,128)(2,1)S(1)}, u32[]{:S(2)}, u32[]{:S(2)}) async-start(bf16[16,3,8,128]{3,2,1,0:T(8,128)(2,1)} %broadcast_select_fusion), calls=%async_computation | async-start | bytes 196608 | tf_op jit(solution)/shard_map/all_to_all | solution.py:121
  26.5 1.8 copy-start.5
  28.3 11.3 %copy-start.4 = (f32[32,8,1024]{2,1,0:T(8,128)S(1)}, f32[32,8,1024]{2,1,0:T(8,128)}, u32[]{:S(2)}) copy-start(f32[32,8,1024]{2,1,0:T(8,128)} %reshape.788) | copy-start | bytes 3145732
  56.8 26.6 %all-to-all-start.1 = ((f32[16,32,512]{2,1,0:T(8,128)}), f32[16,32,512]{2,1,0:T(8,128)S(1)}, u32[]{:S(2)}, u32[]{:S(2)}) async-start(f32[16,32,512]{2,1,0:T(8,128)} %copy.36), calls=%async_computation.1 | async-start | bytes 2097152 | tf_op jit(solution)/shard_map/all_to_all | solution.py:159
  60.5 1007.0 %reduce-scatter.4.cloned.1.call-start = ((), (), s32[]{:S(2)}) async-start(), calls=%async_computation.3 | async-start | bytes 278528
  95.0 2.8 copy-start.2
  313.9 9.0 copy-start.1
  537.9 9.0 copy-start.1
  761.9 9.0 copy-start.1
  985.9 9.0 copy-start.1
  1004.7 5.1 copy-start.3
Sparse Core Ops, SparseCore 0:
  1009.9 57.4 reduce-scatter.3
where the time goes:
time: 1090 us; the launch traced here: 1080 us
  other arithmetic  410 us (38%)
  loops' own time  341 us (31%)
  local copies, waits for them, and re-layouts  134 us (12%)
  matrix products  82.6 us (8%)
  waiting for transfers between devices  82.4 us (8%)
  between operations  14.5 us (1%)
  starting transfers between devices  11.1 us (1%)
    another operation x4, loops' own time, outer_step(): carried, legendre_block = lax.scan(inner_step, carried, degrees, unroll=8)  341 us
    eq x64, other arithmetic, inner_step(): degree == order_int  328 us
    while x448, other arithmetic  55 us
    unnamed x2, waiting for transfers between devices  53.4 us
    dynamic_update_slice x64, local copies, waits for them, and re-layouts, outer_step(): carried, legendre_block = lax.scan(inner_step, carried, degrees, unroll=8)  46.4 us
    slice x64, local copies, waits for them, and re-layouts, outer_step(): carried, legendre_block = lax.scan(inner_step, carried, degrees, unroll=8)  39.6 us
    dot_general x4, matrix products, outer_step(): jnp.einsum('nrl,rlc->rnc', legendre_block, odd_part, precision=lax.Precis...  33 us
    dot_general x4, matrix products, outer_step(): jnp.einsum('nrl,rlc->rnc', legendre_block, even_part, precision=lax.Preci...  26.9 us
  transfers between devices with their start and end apart: 3, of which 3 were waited for; matrix products, arithmetic and copies ran while one was open for 1% of the time, Pallas kernels for 0%

commit v1 on v0

v1 whole, which is shorter than its diff:
```python
import math

import jax
import jax.numpy as jnp
from jax import lax
from jax.experimental import pallas as pl
from jax.experimental.pallas import tpu as pltpu
from jax.sharding import PartitionSpec as P

LATS = 512
LONS = 1024
WAVES = 512
DEG_BLOCK = 128
STEPS = 8


def gauss_half(lat_count):
    index_vals = jnp.arange(lat_count // 2, dtype=jnp.float32)
    theta = math.pi * (4.0 * index_vals + 3.0) / (4.0 * lat_count + 2.0)
    mu_nodes = (1.0 - (lat_count - 1.0) / (8.0 * float(lat_count) ** 3)) * jnp.cos(theta)
    weights = math.pi / (lat_count + 0.5) * jnp.sqrt(1.0 - mu_nodes * mu_nodes)
    return (mu_nodes, weights)


def dft_tables(wave_vals, lon_count):
    longitude = jnp.arange(lon_count, dtype=jnp.int32)
    phase_int = wave_vals[:, None] * longitude[None, :] % lon_count
    angles = phase_int.astype(jnp.float32) * (2.0 * math.pi / lon_count)
    norm_factor = 1.0 / math.sqrt(lon_count)
    return (jnp.cos(angles) * norm_factor, -jnp.sin(angles) * norm_factor)


def dot_nt(left, right):
    return lax.dot_general(
        left, right, (((1,), (1,)), ((), ())), preferred_element_type=jnp.float32
    )


def split_pair(values):
    high = values.astype(jnp.bfloat16)
    low = (values - high.astype(jnp.float32)).astype(jnp.bfloat16)
    return high, low


def legendre_kernel(
    order_ref, first_ref, second_ref, start_ref, mu_ref, parts_ref, out_ref, even_half, odd_half
):
    rows = order_ref.shape[0]
    half = mu_ref.shape[1]
    total_n = first_ref.shape[1]
    cols = out_ref.shape[1]
    order_wide = jnp.broadcast_to(order_ref[...], (rows, half))
    mu_row = jnp.broadcast_to(mu_ref[...], (8, half))
    mu_wide = jnp.concatenate([mu_row] * (rows // 8), axis=0)

    def block_step(block, carried):
        base = pl.multiple_of(block * DEG_BLOCK, DEG_BLOCK)

        def chunk_step(chunk, state):
            current, previous, log_shift = state
            turn = lax.rem(DEG_BLOCK - chunk * STEPS, DEG_BLOCK)
            first = pltpu.roll(first_ref[:, pl.ds(base, DEG_BLOCK)], turn, 1)
            second = pltpu.roll(second_ref[:, pl.ds(base, DEG_BLOCK)], turn, 1)
            scale = jnp.exp(start_ref[...] + log_shift)
            for step in range(STEPS):
                degree = base + chunk * STEPS + step
                coef_first = jnp.broadcast_to(first[:, step : step + 1], (rows, half))
                coef_second = jnp.broadcast_to(second[:, step : step + 1], (rows, half))
                fresh = coef_first * (mu_wide * current - coef_second * previous)
                fresh = jnp.where(order_wide == degree, 1.0, fresh)
                legendre = fresh * scale
                place = pl.ds(chunk * STEPS + step, rows, stride=DEG_BLOCK)
                even_half[place, :] = legendre[:, : half // 2]
                odd_half[place, :] = legendre[:, half // 2 :]
                previous = current
                current = fresh
            too_large = jnp.abs(current) > 2.0**50
            factor = jnp.where(too_large, 2.0 ** (-50), 1.0)
            log_shift = log_shift + jnp.where(too_large, 50.0 * math.log(2.0), 0.0)
            return current * factor, previous * factor, log_shift

        carried = lax.fori_loop(0, DEG_BLOCK // STEPS, chunk_step, carried)

        def wave_step(wave, unused):
            place = pl.ds(pl.multiple_of(wave * DEG_BLOCK, DEG_BLOCK), DEG_BLOCK)
            table = jnp.concatenate([even_half[place, :], odd_half[place, :]], axis=1)
            high, low = split_pair(table)
            part_high, part_low = split_pair(parts_ref[wave])
            with_high = dot_nt(jnp.concatenate([part_high, part_low], axis=0), high)
            with_low = dot_nt(part_high, low)
            both = with_high[: 2 * cols] + with_high[2 * cols :] + with_low
            degrees = base + lax.broadcasted_iota(jnp.int32, (cols, DEG_BLOCK), 1)
            order = jnp.broadcast_to(order_ref[pl.ds(wave, 1), :], (cols, DEG_BLOCK))
            parity = ((degrees + order) & 1) == 0
            out_ref[wave, :, pl.ds(base, DEG_BLOCK)] = jnp.where(parity, both[:cols], both[cols:])
            return unused

        lax.fori_loop(0, rows, wave_step, 0, unroll=4)
        return carried

    zero = jnp.zeros((rows, half), jnp.float32)
    lax.fori_loop(0, total_n // DEG_BLOCK, block_step, (zero, zero, zero))


def legendre_project(wave_vals, fourier, total_n):
    row_count, col_count, lat_count = fourier.shape
    half_lat = lat_count // 2
    mu_nodes, weights = gauss_half(lat_count)
    lat_scale = (weights * math.sqrt(lat_count))[None, None, :]
    north_rows = fourier[:, :, :half_lat]
    south_rows = fourier[:, :, half_lat:][:, :, ::-1]
    even_part = (north_rows + south_rows) * lat_scale
    odd_part = (north_rows - south_rows) * lat_scale
    parts = jnp.concatenate([even_part, odd_part], axis=1)
    order_f = wave_vals.astype(jnp.float32)[:, None]
    sinus = jnp.sqrt(1.0 - mu_nodes * mu_nodes)[None, :]
    start_log = 0.5 * (
        jnp.log(order_f + 0.5)
        + lax.lgamma(order_f + 0.5)
        - lax.lgamma(order_f + 1.0)
        - 0.5 * math.log(math.pi)
    ) + order_f * jnp.log(sinus)
    degree_f = jnp.arange(total_n, dtype=jnp.float32)[None, :]
    coef_first = jnp.sqrt(
        jnp.maximum(4.0 * degree_f * degree_f - 1.0, 1.0)
        / jnp.maximum(degree_f * degree_f - order_f * order_f, 1.0)
    )
    coef_second = jnp.sqrt(
        jnp.maximum((degree_f - 1.0) ** 2 - order_f * order_f, 0.0)
        / jnp.maximum(4.0 * (degree_f - 1.0) ** 2 - 1.0, 1.0)
    )
    return pl.pallas_call(
        legendre_kernel,
        out_shape=jax.ShapeDtypeStruct((row_count, col_count, total_n), jnp.float32),
        in_specs=[pl.BlockSpec(memory_space=pltpu.VMEM)] * 6,
        out_specs=pl.BlockSpec(memory_space=pltpu.VMEM),
        scratch_shapes=[pltpu.VMEM((row_count * DEG_BLOCK, half_lat // 2), jnp.float32)] * 2,
        compiler_params=pltpu.CompilerParams(vmem_limit_bytes=48 * 1024 * 1024),
        name="legendre",
    )(wave_vals[:, None], coef_first, coef_second, start_log, mu_nodes[None, :], parts)


def energy_terms(wave_vals, spectra, levels):
    row_count = spectra.shape[0]
    total_n = spectra.shape[2]
    squares = (spectra * spectra).reshape(row_count, 2, 2, levels, total_n)
    summed = jnp.sum(squares, axis=(1, 2))
    weights = jnp.where(wave_vals == 0, 1.0, 2.0).astype(jnp.float32)
    degree_f = jnp.arange(total_n, dtype=jnp.float32)
    return (
        jnp.sum(summed * weights[:, None, None], axis=0) / (2.0 * (2.0 * degree_f + 1.0))[None, :]
    )


def shards(cell_values, slot_block, slot_counts, slot_tile, remap_tiles, wave_order):
    peer_count = lax.axis_size("band")
    band_index = lax.axis_index("band")
    field_rows, cell_dev = cell_values.shape
    capacity = slot_block.shape[2]
    block_cells = remap_tiles.shape[3]
    tile_width = remap_tiles.shape[4]
    lat_dev = LATS // peer_count
    tile_dev = lat_dev * (LONS // tile_width)
    wave_dev = WAVES // peer_count
    blocks = cell_values.reshape(field_rows, cell_dev // block_cells, block_cells).transpose(
        1, 0, 2
    )
    picked = blocks[slot_block[0]]
    is_valid = jnp.arange(capacity, dtype=jnp.int32)[None, :] < slot_counts[0][:, None]
    picked = jnp.where(is_valid[:, :, None, None], picked, jnp.zeros_like(picked))
    arrived = lax.all_to_all(picked, "band", split_axis=0, concat_axis=0, tiled=True)
    contribs = jnp.einsum(
        "skfc,skcg->skfg", arrived, remap_tiles[0], preferred_element_type=jnp.float32
    )
    tile_ids = slot_tile[0].reshape(-1)
    onehot = (jnp.arange(tile_dev, dtype=jnp.int32)[:, None] == tile_ids[None, :]).astype(
        jnp.float32
    )
    assembled = jnp.dot(
        onehot,
        contribs.reshape(-1, field_rows * tile_width),
        precision=lax.Precision.HIGHEST,
        preferred_element_type=jnp.float32,
    )
    lat_field = (
        assembled.reshape(lat_dev, LONS // tile_width, field_rows, tile_width)
        .transpose(2, 0, 1, 3)
        .reshape(field_rows * lat_dev, LONS)
    )
    cosine, sine_table = dft_tables(wave_order, LONS)
    dims = (((1,), (1,)), ((), ()))
    real_part = lax.dot_general(
        cosine, lat_field, dims, precision=lax.Precision.HIGH, preferred_element_type=jnp.float32
    )
    imag_part = lax.dot_general(
        sine_table,
        lat_field,
        dims,
        precision=lax.Precision.HIGH,
        preferred_element_type=jnp.float32,
    )
    fourier = jnp.concatenate([real_part, imag_part], axis=1)
    regrouped = lax.all_to_all(fourier, "band", split_axis=0, concat_axis=0, tiled=True)
    regrouped = (
        regrouped.reshape(peer_count, wave_dev, 2 * field_rows, lat_dev)
        .transpose(1, 2, 0, 3)
        .reshape(wave_dev, 2 * field_rows, LATS)
    )
    local_waves = lax.dynamic_slice_in_dim(wave_order, band_index * wave_dev, wave_dev, 0)
    spectra = legendre_project(local_waves, regrouped, WAVES)
    partial_value = energy_terms(local_waves, spectra, field_rows // 2)
    levels = field_rows // 2
    shared = partial_value.reshape(levels, peer_count, WAVES // peer_count).transpose(1, 0, 2)
    shared = lax.all_to_all(shared, "band", split_axis=0, concat_axis=0, tiled=True)
    energy = jnp.sum(shared, axis=0)
    return (spectra.reshape(wave_dev, 2, field_rows, WAVES), energy)


def solution(mesh):
    in_specs = (
        P("groups", "band"),
        P("band", None, None),
        P("band", None),
        P("band", None, None),
        P("band", None, None, None, None),
        P(),
    )
    out_specs = (P(("groups", "band"), None, None, None), P("groups", "band"))
    return jax.shard_map(shards, mesh=mesh, in_specs=in_specs, out_specs=out_specs, check_vma=False)
```

time: 1090 us -> 140 us (0.13); the launches traced: 1080 us -> 139 us
  other arithmetic: 410 us -> 9.08 us
  loops' own time: 341 us -> 0 us
  local copies, waits for them, and re-layouts: 134 us -> 19.8 us
  matrix products: 82.6 us -> 18.9 us
  waiting for transfers between devices: 82.4 us -> 28.5 us
  Pallas kernels: 0 us -> 37.6 us
  between operations: 14.5 us -> 0.84 us
  blocking collectives: 0 us -> 13 us
    another operation x5 -> x0, loops' own time: 341 us -> none  [the longest x4 341 us: outer_step(): carried, legendre_block = lax.scan(inner_step, carried, degrees, unroll=8)]
    eq x68 -> x0, other arithmetic: 328 us -> none  [the longest x64 328 us: inner_step(): degree == order_int]
    dot_general x9 -> x1, matrix products: 71.1 us -> 8.94 us  [shards(): lax.dot_general(cosine, lat_field, dims, precision=lax.Precision.HIGH, pr...]
    while x448 -> x0, other arithmetic: 55 us -> none
    unnamed x2 -> x0, waiting for transfers between devices: 53.4 us -> none
    dynamic_update_slice x64 -> x0, local copies, waits for them, and re-layouts: 46.4 us -> none  [outer_step(): carried, legendre_block = lax.scan(inner_step, carried, degrees, unroll=8)]
    slice x65 -> x1, local copies, waits for them, and re-layouts: 41.5 us -> 0.04 us  [legendre_project(): south_rows = fourier[:, :, half_lat:][:, :, ::-1]]
    pallas_call x0 -> x1, Pallas kernels: none -> 37.6 us  [legendre_project(): pl.pallas_call(legendre_kernel, out_shape=jax.ShapeDtypeStruct((row_count...]
  transfers between devices with their start and end apart: 3 -> 2, of which waited for: 3 -> 2; matrix products, arithmetic and copies ran while one was open for 1% -> 1% of each run, Pallas kernels for 0% -> 0%
where the time goes in v1:
time: 140 us; the launch traced here: 139 us
  Pallas kernels  37.6 us (27%)
  waiting for transfers between devices  28.5 us (20%)
  local copies, waits for them, and re-layouts  19.8 us (14%)
  matrix products  18.9 us (13%)
  blocking collectives  13 us (9%)
  starting transfers between devices  11.3 us (8%)
  other arithmetic  9.08 us (6%)
    pallas_call x1, Pallas kernels, legendre_project(): pl.pallas_call(legendre_kernel, out_shape=jax.ShapeDtypeStruct((row_count...  37.6 us
    all_to_all x1, waiting for transfers between devices, shards(): lax.all_to_all(fourier, 'band', split_axis=0, concat_axis=0, tiled=True)  22 us
    all_to_all x1, blocking collectives, shards(): lax.all_to_all(shared, 'band', split_axis=0, concat_axis=0, tiled=True)  13 us
    dot_general x1, matrix products, shards(): lax.dot_general(cosine, lat_field, dims, precision=lax.Precision.HIGH, pr...  8.94 us
    dot_general x1, matrix products, shards(): lax.dot_general(sine_table, lat_field, dims, precision=lax.Precision.HIGH...  8.83 us
    all_to_all x1, starting transfers between devices, shards(): lax.all_to_all(picked, 'band', split_axis=0, concat_axis=0, tiled=True)  7.39 us
    transpose x1, local copies, waits for them, and re-layouts, shards(): regrouped = regrouped.reshape(peer_count, wave_dev, 2 * field_rows, lat_d...  6.58 us
    all_to_all x1, waiting for transfers between devices, shards(): lax.all_to_all(picked, 'band', split_axis=0, concat_axis=0, tiled=True)  6.55 us
  transfers between devices with their start and end apart: 2, of which 2 were waited for; matrix products, arithmetic and copies ran while one was open for 1% of the time, Pallas kernels for 0%

profile of v1, /device:TPU:0, one launch (start us, length us, event | category | flops | bytes accessed | tf_op | source)
XLA Modules:
  0.0 139.1 jit_solution(9318642270997057631)
XLA Ops:
  0.6 0.8 compare_select_fusion
  1.6 0.7 iota_compare_fusion
  2.4 1.6 %gather_fusion = bf16[48,8,128]{2,1,0:T(8,128)(2,1)S(1)} fusion(bf16[128,8,128]{2,1,0:T(8,128)(2,1)} %bitcast.59, s32[1024]{0:T(1024)S(1)} %pad_clamp_fusion), kind=kCustom, calls=%fused_computation | custom fusion | bytes 196800 | tf_op jit(solution)/shard_map/gather | solution.py:168
  3.9 0.8 broadcast_select_fusion
  4.7 7.4 %all-to-all-start = ((bf16[16,3,8,128]{3,2,1,0:T(8,128)(2,1)}), bf16[16,3,8,128]{3,2,1,0:T(8,128)(2,1)S(1)}, u32[]{:S(2)}, u32[]{:S(2)}) async-start(bf16[16,3,8,128]{3,2,1,0:T(8,128)(2,1)} %broadcast_select_fusion), calls=%async_computation | async-start | bytes 196608 | tf_op jit(solution)/shard_map/all_to_all | solution.py:171
  12.1 0.8 copy.50
  12.9 6.5 %all-to-all-done = bf16[16,3,8,128]{3,2,1,0:T(8,128)(2,1)S(1)} async-done(((bf16[16,3,8,128]{3,2,1,0:T(8,128)(2,1)}), bf16[16,3,8,128]{3,2,1,0:T(8,128)(2,1)S(1)}, u32[]{:S(2)}, u32[]{:S(2)}) %all-to-all-start) | async-done | bytes 98336 | tf_op jit(solution)/shard_map/all_to_all | solution.py:171
  20.0 0.6 convolution_bitcast_fusion
  20.7 8.8 %fusion.3 = f32[512,256]{0,1:T(8,128)S(1)} fusion(s32[512]{0:T(512)S(1)} %copy-done.1, f32[32,8,8,128]{3,2,1,0:T(8,128)S(1)} %bitcast.55), kind=kOutput, calls=%fused_computation.7 | convolution fusion | flops 813694976 | bytes 1574912 | tf_op jit(solution)/shard_map/dot_general | solution.py:195
  29.6 8.9 %fusion.7 = f32[512,256]{0,1:T(8,128)S(1)} fusion(s32[512]{0:T(512)S(1)} %copy-done.1, f32[32,8,8,128]{3,2,1,0:T(8,128)S(1)} %bitcast.56), kind=kOutput, calls=%fused_computation.11 | convolution fusion | flops 813170688 | bytes 1574912 | tf_op jit(solution)/shard_map/dot_general | solution.py:192
  38.6 1.3 copy.54
  39.9 3.9 %all-to-all-start.1 = ((f32[16,32,512]{2,1,0:T(8,128)}), f32[16,32,512]{2,1,0:T(8,128)S(1)}, u32[]{:S(2)}, u32[]{:S(2)}) async-start(f32[16,32,512]{2,1,0:T(8,128)} %bitcast.54), calls=%async_computation.1 | async-start | bytes 2097152 | tf_op jit(solution)/shard_map/all_to_all | solution.py:203
  44.5 22.0 %all-to-all-done.1 = f32[16,32,512]{2,1,0:T(8,128)S(1)} async-done(((f32[16,32,512]{2,1,0:T(8,128)}), f32[16,32,512]{2,1,0:T(8,128)S(1)}, u32[]{:S(2)}, u32[]{:S(2)}) %all-to-all-start.1) | async-done | bytes 1048608 | tf_op jit(solution)/shard_map/all_to_all | solution.py:203
  66.5 2.5 %reshape.312 = f32[16,32,16,32]{3,2,1,0:T(8,128)} reshape(f32[16,32,512]{2,1,0:T(8,128)S(1)} %all-to-all-done.1) | data formatting | bytes 2097152 | tf_op jit(solution)/shard_map/reshape | solution.py:205
  69.0 6.6 %copy.55 = f32[32,16,16,32]{3,2,1,0:T(8,128)} copy(f32[32,16,16,32]{3,1,0,2:T(8,128)} %bitcast.52) | data formatting | bytes 2097152 | tf_op jit(solution)/shard_map/transpose | solution.py:206
  75.5 3.5 %reshape.313 = f32[32,16,512]{2,1,0:T(8,128)S(1)} reshape(f32[32,16,16,32]{3,2,1,0:T(8,128)} %copy.55) | data formatting | bytes 2097152 | tf_op jit(solution)/shard_map/reshape | solution.py:207
  79.1 1.0 rev.3
  80.2 1.2 add_multiply_fusion
  81.5 37.6 %legendre.1 = f32[32,16,512]{2,1,0:T(8,128)} custom-call(s32[32,1]{1,0:T(8,128)S(1)} %copy.56.order_ref, f32[32,512]{1,0:T(8,128)S(1)} %get-tuple-element.9.first_ref, f32[32,512]{1,0:T(8,128)S(1)} %get-tuple-element.8.second_ref, f32[32,256]{1,0:T(8,128)S(1)} %multiply_add_fusion.start_ref, f32[1,256]{1,0:T(1,128)S(1)} %cosine_multiply_fusion.mu_ref, ...), custom_call_target="tpu_custom_call" | custom-call | tf_op jit(solution)/shard_map/legendre/pallas_call | solution.py:132
  119.1 1.9 %mul.245 = f32[32,16,512]{2,1,0:T(8,128)S(1)} multiply(f32[32,16,512]{2,1,0:T(8,128)} %legendre.1, f32[32,16,512]{2,1,0:T(8,128)} %legendre.1) | non-fusion elementwise | flops 262144 | bytes 3145728 | tf_op jit(solution)/shard_map/mul | solution.py:146
  121.0 1.3 reshape.315
  122.3 1.6 %reduce_sum.29 = f32[32,4,512]{2,1,0:T(4,128)S(1)} reduce(f32[32,2,2,4,512]{4,3,2,1,0:T(4,128)} %reshape.315, f32[]{:T(128)} %constant.50.clone.1), dimensions={1,2}, to_apply=%region_0.1 | reduce | flops 196608 | bytes 1310724 | tf_op jit(solution)/shard_map/reduce_sum | solution.py:147
  124.2 13.0 %all_to_all.19 = f32[16,1,128]{2,1,0:T(1,128)S(1)} all-to-all(f32[16,1,128]{2,1,0:T(1,128)S(1)} %reshape.327), channel_id=1, replica_groups=mesh['groups'=2,'band'=16] {'band'}, dimensions={0} | all-to-all | bytes 16384 | tf_op jit(solution)/shard_map/all_to_all | solution.py:214
  137.7 0.7 reduce
  (34 shorter events, 3.3 us)
Async XLA Ops:
  0.6 18.9 %copy-start = (bf16[1,16,3,128,128]{4,3,2,1,0:T(8,128)(2,1)S(1)}, bf16[1,16,3,128,128]{4,3,2,1,0:T(8,128)(2,1)}, u32[]{:S(2)}) copy-start(bf16[1,16,3,128,128]{4,3,2,1,0:T(8,128)(2,1)} %param.10) | copy-start | bytes 4718596
  4.7 14.8 %all-to-all-start = ((bf16[16,3,8,128]{3,2,1,0:T(8,128)(2,1)}), bf16[16,3,8,128]{3,2,1,0:T(8,128)(2,1)S(1)}, u32[]{:S(2)}, u32[]{:S(2)}) async-start(bf16[16,3,8,128]{3,2,1,0:T(8,128)(2,1)} %broadcast_select_fusion), calls=%async_computation | async-start | bytes 196608 | tf_op jit(solution)/shard_map/all_to_all | solution.py:171
  20.0 0.7 copy-start.1
  39.9 26.6 %all-to-all-start.1 = ((f32[16,32,512]{2,1,0:T(8,128)}), f32[16,32,512]{2,1,0:T(8,128)S(1)}, u32[]{:S(2)}, u32[]{:S(2)}) async-start(f32[16,32,512]{2,1,0:T(8,128)} %bitcast.54), calls=%async_computation.1 | async-start | bytes 2097152 | tf_op jit(solution)/shard_map/all_to_all | solution.py:203

commit v2 on v1

v2 whole, which is shorter than its diff:
```python
import math

import jax
import jax.numpy as jnp
from jax import lax
from jax.experimental import pallas as pl
from jax.experimental.pallas import tpu as pltpu
from jax.sharding import PartitionSpec as P

LATS = 512
LONS = 1024
WAVES = 512
DEG_BLOCK = 128
STEPS = 8


def gauss_half(lat_count):
    index_vals = jnp.arange(lat_count // 2, dtype=jnp.float32)
    theta = math.pi * (4.0 * index_vals + 3.0) / (4.0 * lat_count + 2.0)
    mu_nodes = (1.0 - (lat_count - 1.0) / (8.0 * float(lat_count) ** 3)) * jnp.cos(theta)
    weights = math.pi / (lat_count + 0.5) * jnp.sqrt(1.0 - mu_nodes * mu_nodes)
    return (mu_nodes, weights)


def dft_tables(wave_vals, lon_count):
    longitude = jnp.arange(lon_count, dtype=jnp.int32)
    phase_int = wave_vals[:, None] * longitude[None, :] % lon_count
    angles = phase_int.astype(jnp.float32) * (2.0 * math.pi / lon_count)
    norm_factor = 1.0 / math.sqrt(lon_count)
    return (jnp.cos(angles) * norm_factor, -jnp.sin(angles) * norm_factor)


def dot_nt(left, right):
    return lax.dot_general(
        left, right, (((1,), (1,)), ((), ())), preferred_element_type=jnp.float32
    )


def split_pair(values):
    high = values.astype(jnp.bfloat16)
    low = (values - high.astype(jnp.float32)).astype(jnp.bfloat16)
    return high, low


def project_kernel(
    order_ref,
    first_ref,
    second_ref,
    start_ref,
    mu_ref,
    lat_scale_ref,
    degree_scale_ref,
    sent_ref,
    out_ref,
    energy_ref,
    left_table,
    right_table,
    landed,
    even_left,
    even_right,
    odd_left,
    odd_right,
    energy_own,
    energy_landed,
    send_sem,
    recv_sem,
    energy_send_sem,
    energy_recv_sem,
):
    peers, lat_dev, width = sent_ref.shape
    rows = order_ref.shape[0]
    half = mu_ref.shape[1]
    total_n = first_ref.shape[1]
    cols = out_ref.shape[1]
    fields = cols // 2
    me = lax.axis_index("band")

    barrier = pltpu.get_barrier_semaphore()
    for hop in range(1, peers):
        peer = lax.rem(me + hop, peers)
        pl.semaphore_signal(
            barrier, inc=1, device_id={"band": peer}, device_id_type=pl.DeviceIdType.MESH
        )
    pl.semaphore_wait(barrier, peers - 1)

    place_me = me + (me // (peers // 2)) * (peers // 2 + peers - 1 - 2 * me)
    landing = pl.ds(pl.multiple_of(place_me * lat_dev, lat_dev), lat_dev)
    copies = []
    for hop in range(1, peers):
        peer = lax.rem(me + hop, peers)
        copy = pltpu.make_async_remote_copy(
            src_ref=sent_ref.at[peer],
            dst_ref=landed.at[landing, :],
            send_sem=send_sem.at[hop],
            recv_sem=recv_sem.at[hop],
            device_id={"band": peer},
            device_id_type=pl.DeviceIdType.MESH,
        )
        copy.start()
        copies.append(copy)
    landed[landing, :] = sent_ref[me]

    order_wide = jnp.broadcast_to(order_ref[...], (rows, half))
    mu_row = jnp.broadcast_to(mu_ref[...], (8, half))
    mu_wide = jnp.concatenate([mu_row] * (rows // 8), axis=0)

    def block_step(block, carried):
        base = pl.multiple_of(block * DEG_BLOCK, DEG_BLOCK)

        def chunk_step(chunk, state):
            current, previous, log_shift = state
            turn = lax.rem(DEG_BLOCK - chunk * STEPS, DEG_BLOCK)
            first = pltpu.roll(first_ref[:, pl.ds(base, DEG_BLOCK)], turn, 1)
            second = pltpu.roll(second_ref[:, pl.ds(base, DEG_BLOCK)], turn, 1)
            scale = jnp.exp(start_ref[...] + log_shift)
            for step in range(STEPS):
                degree = base + chunk * STEPS + step
                coef_first = jnp.broadcast_to(first[:, step : step + 1], (rows, half))
                coef_second = jnp.broadcast_to(second[:, step : step + 1], (rows, half))
                fresh = coef_first * (mu_wide * current - coef_second * previous)
                fresh = jnp.where(order_wide == degree, 1.0, fresh)
                legendre = fresh * scale
                place = pl.ds(degree, rows, stride=total_n)
                left_table[place, :] = legendre[:, : half // 2]
                right_table[place, :] = legendre[:, half // 2 :]
                previous = current
                current = fresh
            too_large = jnp.abs(current) > 2.0**50
            factor = jnp.where(too_large, 2.0 ** (-50), 1.0)
            log_shift = log_shift + jnp.where(too_large, 50.0 * math.log(2.0), 0.0)
            return current * factor, previous * factor, log_shift

        return lax.fori_loop(0, DEG_BLOCK // STEPS, chunk_step, carried)

    zero = jnp.zeros((rows, half), jnp.float32)
    lax.fori_loop(0, total_n // DEG_BLOCK, block_step, (zero, zero, zero))

    for copy in copies:
        copy.wait()

    lat_scale = lat_scale_ref[...]
    for group in range(width // 128):
        span = pl.ds(group * 128, 128)
        north = landed[pl.ds(0, half), span]
        south = landed[pl.ds(half, half), span]
        even = (north + south).T * lat_scale
        odd = (north - south).T * lat_scale
        even_left[span, :] = even[:, : half // 2]
        even_right[span, :] = even[:, half // 2 :]
        odd_left[span, :] = odd[:, : half // 2]
        odd_right[span, :] = odd[:, half // 2 :]

    degrees = lax.broadcasted_iota(jnp.int32, (cols, total_n), 1)

    def gather_rows(ref, wave):
        return jnp.concatenate(
            [
                ref[pl.ds(wave, fields, stride=2 * rows), :],
                ref[pl.ds(wave + rows, fields, stride=2 * rows), :],
            ],
            axis=0,
        )

    def wave_step(wave, total):
        place = pl.ds(pl.multiple_of(wave * total_n, total_n), total_n)
        high, low = split_pair(jnp.concatenate([left_table[place, :], right_table[place, :]], axis=1))
        even = jnp.concatenate([gather_rows(even_left, wave), gather_rows(even_right, wave)], axis=1)
        odd = jnp.concatenate([gather_rows(odd_left, wave), gather_rows(odd_right, wave)], axis=1)
        part_high, part_low = split_pair(jnp.concatenate([even, odd], axis=0))
        with_high = dot_nt(jnp.concatenate([part_high, part_low], axis=0), high)
        with_low = dot_nt(part_high, low)
        both = with_high[: 2 * cols] + with_high[2 * cols :] + with_low
        order = jnp.broadcast_to(order_ref[pl.ds(wave, 1), :], (cols, total_n))
        parity = ((degrees + order) & 1) == 0
        spectrum = jnp.where(parity, both[:cols], both[cols:])
        out_ref[wave] = spectrum
        squares = spectrum * spectrum
        weight = jnp.where(order[:fields] == 0, 1.0, 2.0)
        return total + (squares[:fields] + squares[fields:]) * weight

    total = lax.fori_loop(
        0, rows, wave_step, jnp.zeros((fields, total_n), jnp.float32), unroll=2
    )
    total = (total + pltpu.roll(total, fields // 2, 0)) * degree_scale_ref[...]
    for group in range(total_n // 128):
        energy_own[group] = total[:, group * 128 : (group + 1) * 128]

    chunk_n = total_n // peers
    copies = []
    for hop in range(1, peers):
        peer = lax.rem(me + hop, peers)
        copy = pltpu.make_async_remote_copy(
            src_ref=energy_own.at[peer * chunk_n // 128],
            dst_ref=energy_landed.at[hop],
            send_sem=energy_send_sem.at[hop],
            recv_sem=energy_recv_sem.at[hop],
            device_id={"band": peer},
            device_id_type=pl.DeviceIdType.MESH,
        )
        copy.start()
        copies.append(copy)
    summed = energy_own[me * chunk_n // 128]
    for hop in range(1, peers):
        copies[hop - 1].wait()
        summed = summed + energy_landed[hop]
    turn = lax.rem(128 - lax.rem(me * chunk_n, 128), 128)
    energy_ref[...] = pltpu.roll(summed, turn, 1)


def legendre_project(wave_vals, sent, total_n, lat_count):
    peers, lat_dev, width = sent.shape
    row_count = wave_vals.shape[0]
    col_count = width // row_count
    half_lat = lat_count // 2
    mu_nodes, weights = gauss_half(lat_count)
    lat_scale = (weights * math.sqrt(lat_count))[None, :]
    order_f = wave_vals.astype(jnp.float32)[:, None]
    sinus = jnp.sqrt(1.0 - mu_nodes * mu_nodes)[None, :]
    start_log = 0.5 * (
        jnp.log(order_f + 0.5)
        + lax.lgamma(order_f + 0.5)
        - lax.lgamma(order_f + 1.0)
        - 0.5 * math.log(math.pi)
    ) + order_f * jnp.log(sinus)
    degree_f = jnp.arange(total_n, dtype=jnp.float32)[None, :]
    coef_first = jnp.sqrt(
        jnp.maximum(4.0 * degree_f * degree_f - 1.0, 1.0)
        / jnp.maximum(degree_f * degree_f - order_f * order_f, 1.0)
    )
    coef_second = jnp.sqrt(
        jnp.maximum((degree_f - 1.0) ** 2 - order_f * order_f, 0.0)
        / jnp.maximum(4.0 * (degree_f - 1.0) ** 2 - 1.0, 1.0)
    )
    degree_scale = 1.0 / (2.0 * (2.0 * degree_f + 1.0))
    return pl.pallas_call(
        project_kernel,
        out_shape=(
            jax.ShapeDtypeStruct((row_count, col_count, total_n), jnp.float32),
            jax.ShapeDtypeStruct((8, 128), jnp.float32),
        ),
        in_specs=[pl.BlockSpec(memory_space=pltpu.VMEM)] * 8,
        out_specs=[pl.BlockSpec(memory_space=pltpu.VMEM)] * 2,
        scratch_shapes=[pltpu.VMEM((row_count * total_n, half_lat // 2), jnp.float32)] * 2
        + [pltpu.VMEM((lat_count, width), jnp.float32)]
        + [pltpu.VMEM((width, half_lat // 2), jnp.float32)] * 4
        + [
            pltpu.VMEM((total_n // 128, 8, 128), jnp.float32),
            pltpu.VMEM((peers, 8, 128), jnp.float32),
        ]
        + [pltpu.SemaphoreType.DMA((peers,))] * 4,
        compiler_params=pltpu.CompilerParams(
            vmem_limit_bytes=48 * 1024 * 1024, collective_id=0, has_side_effects=True
        ),
        name="project",
    )(
        wave_vals[:, None],
        coef_first,
        coef_second,
        start_log,
        mu_nodes[None, :],
        lat_scale,
        degree_scale,
        sent,
    )


def shards(cell_values, slot_block, slot_counts, slot_tile, remap_tiles, wave_order):
    peer_count = lax.axis_size("band")
    band_index = lax.axis_index("band")
    field_rows, cell_dev = cell_values.shape
    capacity = slot_block.shape[2]
    block_cells = remap_tiles.shape[3]
    tile_width = remap_tiles.shape[4]
    lat_dev = LATS // peer_count
    tile_dev = lat_dev * (LONS // tile_width)
    wave_dev = WAVES // peer_count
    blocks = cell_values.reshape(field_rows, cell_dev // block_cells, block_cells).transpose(
        1, 0, 2
    )
    picked = blocks[slot_block[0]]
    is_valid = jnp.arange(capacity, dtype=jnp.int32)[None, :] < slot_counts[0][:, None]
    picked = jnp.where(is_valid[:, :, None, None], picked, jnp.zeros_like(picked))
    arrived = lax.all_to_all(picked, "band", split_axis=0, concat_axis=0, tiled=True)
    contribs = jnp.einsum(
        "skfc,skcg->skfg", arrived, remap_tiles[0], preferred_element_type=jnp.float32
    )
    tiles_lat = LONS // tile_width
    tile_ids = slot_tile[0].reshape(-1)
    backward = (lat_dev - 1 - tile_ids // tiles_lat) * tiles_lat + tile_ids % tiles_lat
    tile_ids = jnp.where(band_index < peer_count // 2, tile_ids, backward)
    onehot = (jnp.arange(tile_dev, dtype=jnp.int32)[:, None] == tile_ids[None, :]).astype(
        jnp.float32
    )
    assembled = jnp.dot(
        onehot,
        contribs.reshape(-1, field_rows * tile_width),
        precision=lax.Precision.HIGHEST,
        preferred_element_type=jnp.float32,
    )
    lat_field = (
        assembled.reshape(lat_dev, LONS // tile_width, field_rows, tile_width)
        .transpose(2, 0, 1, 3)
        .reshape(field_rows * lat_dev, LONS)
    )
    cosine, sine_table = dft_tables(wave_order, LONS)
    table = jnp.concatenate(
        [cosine.reshape(peer_count, wave_dev, LONS), sine_table.reshape(peer_count, wave_dev, LONS)],
        axis=1,
    ).reshape(2 * WAVES, LONS)
    fourier = lax.dot_general(
        lat_field,
        table,
        (((1,), (1,)), ((), ())),
        precision=lax.Precision.HIGH,
        preferred_element_type=jnp.float32,
    )
    sent = (
        fourier.reshape(field_rows, lat_dev, peer_count, 2 * wave_dev)
        .transpose(2, 1, 0, 3)
        .reshape(peer_count, lat_dev, 2 * field_rows * wave_dev)
    )
    local_waves = lax.dynamic_slice_in_dim(wave_order, band_index * wave_dev, wave_dev, 0)
    spectra, energy = legendre_project(local_waves, sent, WAVES, LATS)
    energy = energy[: field_rows // 2, : WAVES // peer_count]
    return (spectra.reshape(wave_dev, 2, field_rows, WAVES), energy)


def solution(mesh):
    in_specs = (
        P("groups", "band"),
        P("band", None, None),
        P("band", None),
        P("band", None, None),
        P("band", None, None, None, None),
        P(),
    )
    out_specs = (P(("groups", "band"), None, None, None), P("groups", "band"))
    return jax.shard_map(shards, mesh=mesh, in_specs=in_specs, out_specs=out_specs, check_vma=False)
```

time: 140 us -> 85 us (0.61)
  waiting for transfers between devices: 28.5 us -> 0.01 us
  blocking collectives: 13 us -> 0 us
  matrix products: 18.9 us -> 8.3 us
  local copies, waits for them, and re-layouts: 19.8 us -> 11.4 us
  other arithmetic: 9.08 us -> 14.2 us
  Pallas kernels: 37.6 us -> 42.6 us
  starting transfers between devices: 11.3 us -> 7.39 us
    all_to_all x1 -> x0, waiting for transfers between devices: 22 us -> none  [shards(): lax.all_to_all(fourier, 'band', split_axis=0, concat_axis=0, tiled=True)]
    all_to_all x1 -> x0, blocking collectives: 13 us -> none  [shards(): lax.all_to_all(shared, 'band', split_axis=0, concat_axis=0, tiled=True)]
    dot_general x2 -> x1, matrix products: 17.8 us -> 6.2 us  [shards(): lax.dot_general(lat_field, table, (((1,), (1,)), ((), ())), precision=lax...]
    mul x5 -> x3, other arithmetic: 3.21 us -> 10.8 us  [the longest x1 10.7 us: dft_tables(): return (jnp.cos(angles) * norm_factor, -jnp.sin(angles) * norm_factor)]
    all_to_all x1, waiting for transfers between devices: 6.55 us -> 0.01 us  [shards(): lax.all_to_all(picked, 'band', split_axis=0, concat_axis=0, tiled=True)]
    reshape x3 -> x1, local copies, waits for them, and re-layouts: 7.32 us -> 1.93 us  [shards(): sent = fourier.reshape(field_rows, lat_dev, peer_count, 2 * wave_dev).tra...]
    pallas_call x1, Pallas kernels: 37.6 us -> 42.6 us  [legendre_project(): pl.pallas_call(project_kernel, out_shape=(jax.ShapeDtypeStruct((row_count...]
    all_to_all x1 -> x0, starting transfers between devices: 3.88 us -> none  [shards(): lax.all_to_all(fourier, 'band', split_axis=0, concat_axis=0, tiled=True)]
  transfers between devices with their start and end apart: 2 -> 1, of which waited for: 2 -> 0; matrix products, arithmetic and copies ran while one was open for 1% -> 16% of each run, Pallas kernels for 0% -> 0%
where the time goes in v2:
time: 85 us; the launch traced here: 84.6 us
  Pallas kernels  42.6 us (50%)
  other arithmetic  14.2 us (17%)
  local copies, waits for them, and re-layouts  11.4 us (13%)
  matrix products  8.3 us (10%)
  starting transfers between devices  7.39 us (9%)
    pallas_call x1, Pallas kernels, legendre_project(): pl.pallas_call(project_kernel, out_shape=(jax.ShapeDtypeStruct((row_count...  42.6 us
    mul x1, other arithmetic, dft_tables(): return (jnp.cos(angles) * norm_factor, -jnp.sin(angles) * norm_factor)  10.7 us
    all_to_all x1, starting transfers between devices, shards(): lax.all_to_all(picked, 'band', split_axis=0, concat_axis=0, tiled=True)  7.39 us
    dot_general x1, matrix products, shards(): lax.dot_general(lat_field, table, (((1,), (1,)), ((), ())), precision=lax...  6.2 us
    transpose x1, local copies, waits for them, and re-layouts, shards(): sent = fourier.reshape(field_rows, lat_dev, peer_count, 2 * wave_dev).tra...  2.97 us
    reshape x1, local copies, waits for them, and re-layouts, shards(): sent = fourier.reshape(field_rows, lat_dev, peer_count, 2 * wave_dev).tra...  1.93 us
  transfers between devices with their start and end apart: 1, of which 0 were waited for; matrix products, arithmetic and copies ran while one was open for 16% of the time, Pallas kernels for 0%

profile of v2, /device:TPU:0, one launch (start us, length us, event | category | flops | bytes accessed | tf_op | source)
XLA Modules:
  0.0 84.6 jit_solution(15520044185792964281)
XLA Ops:
  0.6 0.8 compare_select_fusion
  1.4 0.1 copy.14
  1.5 0.1 reshape.386
  1.6 0.7 iota_compare_fusion
  2.4 1.6 %gather_fusion = bf16[48,8,128]{2,1,0:T(8,128)(2,1)S(1)} fusion(bf16[128,8,128]{2,1,0:T(8,128)(2,1)} %bitcast.58, s32[1024]{0:T(1024)S(1)} %pad_clamp_fusion), kind=kCustom, calls=%fused_computation | custom fusion | bytes 196800 | tf_op jit(solution)/shard_map/gather | solution.py:280
  3.9 0.8 broadcast_select_fusion
  4.7 7.4 %all-to-all-start = ((bf16[16,3,8,128]{3,2,1,0:T(8,128)(2,1)}), bf16[16,3,8,128]{3,2,1,0:T(8,128)(2,1)S(1)}, u32[]{:S(2)}, u32[]{:S(2)}) async-start(bf16[16,3,8,128]{3,2,1,0:T(8,128)(2,1)} %broadcast_select_fusion), calls=%async_computation | async-start | bytes 196608 | tf_op jit(solution)/shard_map/all_to_all | solution.py:283
  12.2 0.8 add_multiply_fusion.1
  13.0 0.8 dynamic-slice_bitcast_fusion
  13.8 0.8 mul.233
  14.6 0.1 copy.18.order_ref
  14.7 10.7 %cosine_multiply_fusion = (f32[16,32,1024]{2,1,0:T(8,128)}, f32[16,32,1024]{2,1,0:T(8,128)}) fusion(s32[16,32]{1,0:T(8,128)S(1)} %mul.233), kind=kLoop, calls=%fused_computation.12 | loop fusion | flops 8912896 | bytes 4196352 | tf_op jit(solution)/shard_map/mul | solution.py:30
  25.4 0.1 copy.13
  25.5 0.1 reshape_squeeze.3
  25.7 0.1 divide_sqrt_fusion
  25.8 0.5 fusion.10
  26.3 1.6 %convolution_bitcast_fusion = f32[8,32,8,128]{3,2,0,1:T(8,128)} fusion(s32[48]{0:T(128)S(1)} %broadcast_select_fusion.1, s32[32,8]{1,0:T(8,128)S(1)} %multiply_add_fusion.1, f32[6,8,8,128]{3,2,1,0:T(8,128)S(1)} %bitcast.56), kind=kOutput, calls=%fused_computation.19 | convolution fusion | flops 151007232 | bytes 1246400 | tf_op jit(solution)/shard_map/dot_general | solution.py:294
  27.9 1.4 %dot_general.19 = f32[8,32,1024]{2,0,1:T(8,128)S(1)} reshape(f32[8,32,8,128]{3,2,0,1:T(8,128)} %convolution_bitcast_fusion) | data formatting | bytes 2097152 | tf_op jit(solution)/shard_map/dot_general | solution.py:310
  29.3 6.2 %fusion.9 = f32[16,32,8,64]{3,1,0,2:T(8,128)S(1)} fusion(f32[16,32,1024]{2,1,0:T(8,128)} %get-tuple-element.9, f32[16,32,1024]{2,1,0:T(8,128)} %get-tuple-element.8, f32[8,32,1024,1]{2,0,1,3:T(8,128)S(1)} %bitcast.55), kind=kOutput, calls=%fused_computation.16 | convolution fusion | flops 1611661312 | bytes 6291456 | tf_op jit(solution)/shard_map/dot_general | solution.py:310
  35.5 3.0 %copy.17 = f32[16,32,8,64]{3,2,1,0:T(8,128)} copy(f32[16,32,8,64]{3,1,0,2:T(8,128)S(1)} %fusion.9) | data formatting | bytes 2097152 | tf_op jit(solution)/shard_map/transpose | solution.py:319
  38.5 1.9 %reshape.382.sent_ref = f32[16,32,512]{2,1,0:T(8,128)S(1)} reshape(f32[16,32,8,64]{3,2,1,0:T(8,128)} %copy.17) | data formatting | bytes 2097152 | tf_op jit(solution)/shard_map/reshape | solution.py:320
  40.4 42.6 %project.1 = (f32[32,16,512]{2,1,0:T(8,128)S(1)}, f32[8,128]{1,0:T(8,128)S(1)}) custom-call(s32[32,1]{1,0:T(8,128)S(1)} %copy.18.order_ref, f32[32,512]{1,0:T(8,128)S(1)} %get-tuple-element.11.first_ref, f32[32,512]{1,0:T(8,128)S(1)} %get-tuple-element.10.second_ref, f32[32,256]{1,0:T(8,128)S(1)} %multiply_add_fusion.start_ref, ...), custom_call_target="tpu_custom_call" | custom-call | tf_op jit(solution)/shard_map/project/pallas_call | solution.py:235
  83.0 0.6 slice.3
  83.6 1.0 %copy.35 = f32[32,2,8,512]{3,2,1,0:T(8,128)} copy(f32[32,2,8,512]{3,2,1,0:T(8,128)S(1)} %bitcast.54) | data formatting | bytes 2097152
  (15 shorter events, 0.3 us)
Async XLA Ops:
  0.6 25.2 %copy-start = (bf16[1,16,3,128,128]{4,3,2,1,0:T(8,128)(2,1)S(1)}, bf16[1,16,3,128,128]{4,3,2,1,0:T(8,128)(2,1)}, u32[]{:S(2)}) copy-start(bf16[1,16,3,128,128]{4,3,2,1,0:T(8,128)(2,1)} %param.10) | copy-start | bytes 4718596
  4.7 21.1 %all-to-all-start = ((bf16[16,3,8,128]{3,2,1,0:T(8,128)(2,1)}), bf16[16,3,8,128]{3,2,1,0:T(8,128)(2,1)S(1)}, u32[]{:S(2)}, u32[]{:S(2)}) async-start(bf16[16,3,8,128]{3,2,1,0:T(8,128)(2,1)} %broadcast_select_fusion), calls=%async_computation | async-start | bytes 196608 | tf_op jit(solution)/shard_map/all_to_all | solution.py:283
  14.7 10.7 %copy-start.1 = (s32[1,16,3]{1,0,2:T(1,128)S(1)}, s32[1,16,3]{1,0,2:T(1,128)}, u32[]{:S(2)}) copy-start(s32[1,16,3]{1,0,2:T(1,128)} %param.9) | copy-start | bytes 580

commit v3 on v2

--- a/solution.py
+++ b/solution.py
@@ -12,6 +12,7 @@
 WAVES = 512
 DEG_BLOCK = 128
 STEPS = 8
+ROW_GAP = 8
 
 
 def gauss_half(lat_count):
@@ -22,12 +23,16 @@
     return (mu_nodes, weights)
 
 
-def dft_tables(wave_vals, lon_count):
-    longitude = jnp.arange(lon_count, dtype=jnp.int32)
-    phase_int = wave_vals[:, None] * longitude[None, :] % lon_count
-    angles = phase_int.astype(jnp.float32) * (2.0 * math.pi / lon_count)
+def dft_base(wave_vals, lon_count, width):
     norm_factor = 1.0 / math.sqrt(lon_count)
-    return (jnp.cos(angles) * norm_factor, -jnp.sin(angles) * norm_factor)
+    step = 2.0 * math.pi / lon_count
+    point = jnp.arange(width, dtype=jnp.int32)
+    start = jnp.arange(0, lon_count, width, dtype=jnp.int32)
+    base = (wave_vals[:, None] * point[None, :] % lon_count).astype(jnp.float32) * step
+    offset = (wave_vals[:, None] * start[None, :] % lon_count).astype(jnp.float32) * step
+    return lax.optimization_barrier(
+        (jnp.cos(base) * norm_factor, jnp.sin(base) * norm_factor, jnp.cos(offset), jnp.sin(offset))
+    )
 
 
 def dot_nt(left, right):
@@ -120,7 +125,7 @@
                 fresh = coef_first * (mu_wide * current - coef_second * previous)
                 fresh = jnp.where(order_wide == degree, 1.0, fresh)
                 legendre = fresh * scale
-                place = pl.ds(degree, rows, stride=total_n)
+                place = pl.ds(degree, rows, stride=total_n + ROW_GAP)
                 left_table[place, :] = legendre[:, : half // 2]
                 right_table[place, :] = legendre[:, half // 2 :]
                 previous = current
@@ -162,7 +167,7 @@
         )
 
     def wave_step(wave, total):
-        place = pl.ds(pl.multiple_of(wave * total_n, total_n), total_n)
+        place = pl.ds(pl.multiple_of(wave * (total_n + ROW_GAP), ROW_GAP), total_n)
         high, low = split_pair(jnp.concatenate([left_table[place, :], right_table[place, :]], axis=1))
         even = jnp.concatenate([gather_rows(even_left, wave), gather_rows(even_right, wave)], axis=1)
         odd = jnp.concatenate([gather_rows(odd_left, wave), gather_rows(odd_right, wave)], axis=1)
@@ -240,7 +245,7 @@
         ),
         in_specs=[pl.BlockSpec(memory_space=pltpu.VMEM)] * 8,
         out_specs=[pl.BlockSpec(memory_space=pltpu.VMEM)] * 2,
-        scratch_shapes=[pltpu.VMEM((row_count * total_n, half_lat // 2), jnp.float32)] * 2
+        scratch_shapes=[pltpu.VMEM((row_count * (total_n + ROW_GAP), half_lat // 2), jnp.float32)] * 2
         + [pltpu.VMEM((lat_count, width), jnp.float32)]
         + [pltpu.VMEM((width, half_lat // 2), jnp.float32)] * 4
         + [
@@ -302,9 +307,11 @@
         .transpose(2, 0, 1, 3)
         .reshape(field_rows * lat_dev, LONS)
     )
-    cosine, sine_table = dft_tables(wave_order, LONS)
+    base_cos, base_sin, offset_cos, offset_sin = dft_base(wave_order, LONS, tile_width)
+    cosine = offset_cos[:, :, None] * base_cos[:, None, :] - offset_sin[:, :, None] * base_sin[:, None, :]
+    sine = offset_sin[:, :, None] * base_cos[:, None, :] + offset_cos[:, :, None] * base_sin[:, None, :]
     table = jnp.concatenate(
-        [cosine.reshape(peer_count, wave_dev, LONS), sine_table.reshape(peer_count, wave_dev, LONS)],
+        [cosine.reshape(peer_count, wave_dev, LONS), -sine.reshape(peer_count, wave_dev, LONS)],
         axis=1,
     ).reshape(2 * WAVES, LONS)
     fourier = lax.dot_general(

time: 85 us -> 84.9 us (level)
  local copies, waits for them, and re-layouts: 11.4 us -> 16 us
  other arithmetic: 14.2 us -> 11 us
  Pallas kernels: 42.6 us -> 41 us
    mul x1 -> x2, other arithmetic: 10.7 us -> 1.8 us  [the longest x1 1.8 us: dft_base(): jnp.sin(base) * norm_factor]
    sub x0 -> x1, other arithmetic: none -> 3.89 us  [shards(): offset_cos[:, :, None] * base_cos[:, None, :]]
    sub x0 -> x1, local copies, waits for them, and re-layouts: none -> 2.72 us  [shards(): offset_cos[:, :, None] * base_cos[:, None, :]]
    neg x0 -> x1, local copies, waits for them, and re-layouts: none -> 2.7 us  [shards(): -sine.reshape(peer_count, wave_dev, LONS)]
    sin x0 -> x1, other arithmetic: none -> 1.78 us  [dft_base(): jnp.sin(offset)]
    pallas_call x1, Pallas kernels: 42.6 us -> 41 us  [legendre_project(): pl.pallas_call(project_kernel, out_shape=(jax.ShapeDtypeStruct((row_count...]
  transfers between devices with their start and end apart: 1 -> 1, of which waited for: 0 -> 0; matrix products, arithmetic and copies ran while one was open for 16% -> 18% of each run, Pallas kernels for 0% -> 0%
where the time goes in v3:
time: 84.9 us; the launch traced here: 84.4 us
  Pallas kernels  41 us (48%)
  local copies, waits for them, and re-layouts  16 us (19%)
  other arithmetic  11 us (13%)
  matrix products  8.3 us (10%)
  starting transfers between devices  7.39 us (9%)
    pallas_call x1, Pallas kernels, legendre_project(): pl.pallas_call(project_kernel, out_shape=(jax.ShapeDtypeStruct((row_count...  41 us
    all_to_all x1, starting transfers between devices, shards(): lax.all_to_all(picked, 'band', split_axis=0, concat_axis=0, tiled=True)  7.39 us
    dot_general x1, matrix products, shards(): lax.dot_general(lat_field, table, (((1,), (1,)), ((), ())), precision=lax...  6.2 us
    sub x1, other arithmetic, shards(): offset_cos[:, :, None] * base_cos[:, None, :]  3.89 us
    transpose x1, local copies, waits for them, and re-layouts, shards(): sent = fourier.reshape(field_rows, lat_dev, peer_count, 2 * wave_dev).tra...  2.97 us
    sub x1, local copies, waits for them, and re-layouts, shards(): offset_cos[:, :, None] * base_cos[:, None, :]  2.72 us
    neg x1, local copies, waits for them, and re-layouts, shards(): -sine.reshape(peer_count, wave_dev, LONS)  2.7 us
    reshape x1, local copies, waits for them, and re-layouts, shards(): sent = fourier.reshape(field_rows, lat_dev, peer_count, 2 * wave_dev).tra...  1.93 us
  transfers between devices with their start and end apart: 1, of which 0 were waited for; matrix products, arithmetic and copies ran while one was open for 18% of the time, Pallas kernels for 0%

profile of v3, /device:TPU:0, one launch (start us, length us, event | category | flops | bytes accessed | tf_op | source)
XLA Modules:
  0.0 84.4 jit_solution(16951850446975413769)
XLA Ops:
  0.6 0.8 compare_select_fusion
  1.6 0.7 iota_compare_fusion
  2.4 1.6 %gather_fusion = bf16[48,8,128]{2,1,0:T(8,128)(2,1)S(1)} fusion(bf16[128,8,128]{2,1,0:T(8,128)(2,1)} %bitcast.58, s32[1024]{0:T(1024)S(1)} %pad_clamp_fusion), kind=kCustom, calls=%fused_computation | custom fusion | bytes 196800 | tf_op jit(solution)/shard_map/gather | solution.py:285
  3.9 0.8 broadcast_select_fusion
  4.7 7.4 %all-to-all-start = ((bf16[16,3,8,128]{3,2,1,0:T(8,128)(2,1)}), bf16[16,3,8,128]{3,2,1,0:T(8,128)(2,1)S(1)}, u32[]{:S(2)}, u32[]{:S(2)}) async-start(bf16[16,3,8,128]{3,2,1,0:T(8,128)(2,1)} %broadcast_select_fusion), calls=%async_computation | async-start | bytes 196608 | tf_op jit(solution)/shard_map/all_to_all | solution.py:288
  12.2 1.8 %sine_multiply_fusion = (f32[512,128]{1,0:T(8,128)S(1)}, f32[512,128]{1,0:T(8,128)S(1)}) fusion(s32[512]{0:T(512)} %param.11), kind=kLoop, calls=%fused_computation.26 | loop fusion | flops 1048576 | bytes 526336 | tf_op jit(solution)/shard_map/mul | solution.py:34
  14.0 0.8 add_multiply_fusion.1
  14.8 0.8 dynamic-slice_bitcast_fusion
  15.7 1.8 %fusion.17 = (f32[512,8]{1,0:T(8,128)S(1)}, f32[512,8]{1,0:T(8,128)S(1)}) fusion(s32[8]{0:T(128)S(1)} %iota_multiply_fusion.1, s32[512]{0:T(512)} %param.11), kind=kLoop, calls=%fused_computation.34 | loop fusion | flops 57344 | bytes 34848 | tf_op jit(solution)/shard_map/sin | solution.py:34
  17.5 3.9 %multiply_subtract_fusion = (f32[512,8,128]{2,1,0:T(8,128)}, f32[512,8,128]{2,1,0:T(8,128)}) fusion(f32[512,128]{1,0:T(8,128)S(1)} %get-tuple-element.11, f32[512,8]{1,0:T(8,128)S(1)} %get-tuple-element.10, f32[512,128]{1,0:T(8,128)S(1)} %get-tuple-element.9, f32[512,8]{1,0:T(8,128)S(1)} %get-tuple-element.8), kind=kLoop, calls=%fused_computation.6 | loop fusion | flops 3670016 | bytes 4751360 | tf_op jit(solution)/shard_map/sub | solution.py:311
  21.4 2.7 %neg.7 = f32[16,32,1024]{2,1,0:T(8,128)} reshape(f32[512,8,128]{2,1,0:T(8,128)} %get-tuple-element.17) | data formatting | bytes 4194304 | tf_op jit(solution)/shard_map/neg | solution.py:314
  24.1 2.7 %sub.99 = f32[16,32,1024]{2,1,0:T(8,128)} reshape(f32[512,8,128]{2,1,0:T(8,128)} %get-tuple-element.16) | data formatting | bytes 4194304 | tf_op jit(solution)/shard_map/sub | solution.py:311
  26.9 0.1 reshape_squeeze.3
  27.0 0.1 copy.18.order_ref
  27.1 0.1 divide_sqrt_fusion
  27.3 0.5 fusion.4
  27.8 1.6 %convolution_bitcast_fusion = f32[8,32,8,128]{3,2,0,1:T(8,128)} fusion(s32[48]{0:T(128)S(1)} %broadcast_select_fusion.1, s32[32,8]{1,0:T(8,128)S(1)} %multiply_add_fusion.1, f32[6,8,8,128]{3,2,1,0:T(8,128)S(1)} %bitcast.56), kind=kOutput, calls=%fused_computation.10 | convolution fusion | flops 151007232 | bytes 1246400 | tf_op jit(solution)/shard_map/dot_general | solution.py:299
  29.4 1.4 %dot_general.19 = f32[8,32,1024]{2,0,1:T(8,128)S(1)} reshape(f32[8,32,8,128]{3,2,0,1:T(8,128)} %convolution_bitcast_fusion) | data formatting | bytes 2097152 | tf_op jit(solution)/shard_map/dot_general | solution.py:317
  30.8 6.2 %fusion.3 = f32[16,32,8,64]{3,1,0,2:T(8,128)S(1)} fusion(f32[16,32,1024]{2,1,0:T(8,128)} %neg.7, f32[16,32,1024]{2,1,0:T(8,128)} %sub.99, f32[8,32,1024,1]{2,0,1,3:T(8,128)S(1)} %bitcast.55), kind=kOutput, calls=%fused_computation.7 | convolution fusion | flops 1611661312 | bytes 6291456 | tf_op jit(solution)/shard_map/dot_general | solution.py:317
  37.0 3.0 %copy.17 = f32[16,32,8,64]{3,2,1,0:T(8,128)} copy(f32[16,32,8,64]{3,1,0,2:T(8,128)S(1)} %fusion.3) | data formatting | bytes 2097152 | tf_op jit(solution)/shard_map/transpose | solution.py:326
  40.0 1.9 %reshape.390.sent_ref = f32[16,32,512]{2,1,0:T(8,128)S(1)} reshape(f32[16,32,8,64]{3,2,1,0:T(8,128)} %copy.17) | data formatting | bytes 2097152 | tf_op jit(solution)/shard_map/reshape | solution.py:327
  41.9 41.0 %project.1 = (f32[32,16,512]{2,1,0:T(8,128)S(1)}, f32[8,128]{1,0:T(8,128)S(1)}) custom-call(s32[32,1]{1,0:T(8,128)S(1)} %copy.18.order_ref, f32[32,512]{1,0:T(8,128)S(1)} %get-tuple-element.23.first_ref, f32[32,512]{1,0:T(8,128)S(1)} %get-tuple-element.22.second_ref, f32[32,256]{1,0:T(8,128)S(1)} %multiply_add_fusion.start_ref, ...), custom_call_target="tpu_custom_call" | custom-call | tf_op jit(solution)/shard_map/project/pallas_call | solution.py:240
  82.9 0.6 slice.3
  83.5 1.0 %copy.35 = f32[32,2,8,512]{3,2,1,0:T(8,128)} copy(f32[32,2,8,512]{3,2,1,0:T(8,128)S(1)} %bitcast.54) | data formatting | bytes 2097152
  (19 shorter events, 0.5 us)
Async XLA Ops:
  0.6 26.7 %copy-start = (bf16[1,16,3,128,128]{4,3,2,1,0:T(8,128)(2,1)S(1)}, bf16[1,16,3,128,128]{4,3,2,1,0:T(8,128)(2,1)}, u32[]{:S(2)}) copy-start(bf16[1,16,3,128,128]{4,3,2,1,0:T(8,128)(2,1)} %param.10) | copy-start | bytes 4718596
  4.7 22.6 %all-to-all-start = ((bf16[16,3,8,128]{3,2,1,0:T(8,128)(2,1)}), bf16[16,3,8,128]{3,2,1,0:T(8,128)(2,1)S(1)}, u32[]{:S(2)}, u32[]{:S(2)}) async-start(bf16[16,3,8,128]{3,2,1,0:T(8,128)(2,1)} %broadcast_select_fusion), calls=%async_computation | async-start | bytes 196608 | tf_op jit(solution)/shard_map/all_to_all | solution.py:288
  24.1 2.7 %copy-start.1 = (s32[1,16,3]{1,0,2:T(1,128)S(1)}, s32[1,16,3]{1,0,2:T(1,128)}, u32[]{:S(2)}) copy-start(s32[1,16,3]{1,0,2:T(1,128)} %param.9) | copy-start | bytes 580

commit v4 on v3

--- a/solution.py
+++ b/solution.py
@@ -23,15 +23,26 @@
     return (mu_nodes, weights)
 
 
-def dft_base(wave_vals, lon_count, width):
+def dft_base(wave_vals, lon_count, width, peers):
     norm_factor = 1.0 / math.sqrt(lon_count)
     step = 2.0 * math.pi / lon_count
     point = jnp.arange(width, dtype=jnp.int32)
     start = jnp.arange(0, lon_count, width, dtype=jnp.int32)
     base = (wave_vals[:, None] * point[None, :] % lon_count).astype(jnp.float32) * step
     offset = (wave_vals[:, None] * start[None, :] % lon_count).astype(jnp.float32) * step
-    return lax.optimization_barrier(
+    cosine, sine, offset_cos, offset_sin = lax.optimization_barrier(
         (jnp.cos(base) * norm_factor, jnp.sin(base) * norm_factor, jnp.cos(offset), jnp.sin(offset))
+    )
+
+    def by_peer(real_rows, imag_rows):
+        both = [rows.reshape(peers, -1, rows.shape[-1]) for rows in (real_rows, imag_rows)]
+        return jnp.concatenate(both, axis=1).reshape(-1, real_rows.shape[-1])
+
+    return (
+        by_peer(cosine, -sine),
+        by_peer(sine, cosine),
+        by_peer(offset_cos, offset_cos),
+        by_peer(offset_sin, offset_sin),
     )
 
 
@@ -45,6 +56,74 @@
     high = values.astype(jnp.bfloat16)
     low = (values - high.astype(jnp.float32)).astype(jnp.bfloat16)
     return high, low
+
+
+def dft_kernel(field_ref, base_c_ref, base_s_ref, offset_c_ref, offset_s_ref, sent_ref):
+    dests, lat_dev, width = sent_ref.shape
+    rows, points = base_c_ref.shape
+    tiles = offset_c_ref.shape[1]
+    fields = field_ref.shape[1] // points
+    per_dest = rows // dests
+    base_c = base_c_ref[...]
+    base_s = base_s_ref[...]
+
+    def tile_field(tile):
+        return jnp.concatenate(
+            [
+                field_ref[tile * lat_dev : (tile + 1) * lat_dev, row * points : (row + 1) * points]
+                for row in range(fields)
+            ],
+            axis=0,
+        )
+
+    def tile_table(tile):
+        offset_c = jnp.broadcast_to(offset_c_ref[:, tile : tile + 1], (rows, points))
+        offset_s = jnp.broadcast_to(offset_s_ref[:, tile : tile + 1], (rows, points))
+        return offset_c * base_c - offset_s * base_s
+
+    height = fields * lat_dev
+    total = jnp.zeros((height, rows), jnp.float32)
+    for tile in range(0, tiles, 2):
+        field = jnp.concatenate([tile_field(tile), tile_field(tile + 1)], axis=1)
+        table = jnp.concatenate([tile_table(tile), tile_table(tile + 1)], axis=1)
+        field_high, field_low = split_pair(field)
+        table_high, table_low = split_pair(table)
+        with_high = dot_nt(jnp.concatenate([field_high, field_low], axis=0), table_high)
+        total = total + (with_high[:height] + with_high[height:] + dot_nt(field_high, table_low))
+    for dest in range(dests):
+        sent_ref[dest] = jnp.concatenate(
+            [
+                total[row * lat_dev : (row + 1) * lat_dev, dest * per_dest : (dest + 1) * per_dest]
+                for row in range(fields)
+            ],
+            axis=1,
+        )
+
+
+def fourier_blocks(field, tables, peers, lat_dev, fields):
+    table_rows, points = tables[0].shape
+    tiles = tables[2].shape[1]
+    block = 256
+    per_dest = table_rows // peers
+    dests = block // per_dest
+    width = fields * per_dest
+    row_block = pl.BlockSpec((block, points), lambda step: (step, 0))
+    offset_block = pl.BlockSpec((block, tiles), lambda step: (step, 0))
+    return pl.pallas_call(
+        dft_kernel,
+        grid=(table_rows // block,),
+        out_shape=jax.ShapeDtypeStruct((peers, lat_dev, width), jnp.float32),
+        in_specs=[
+            pl.BlockSpec(field.shape, lambda step: (0, 0)),
+            row_block,
+            row_block,
+            offset_block,
+            offset_block,
+        ],
+        out_specs=pl.BlockSpec((dests, lat_dev, width), lambda step: (step, 0, 0)),
+        compiler_params=pltpu.CompilerParams(vmem_limit_bytes=32 * 1024 * 1024),
+        name="fourier",
+    )(field, *tables)
 
 
 def project_kernel(
@@ -291,8 +370,9 @@
     )
     tiles_lat = LONS // tile_width
     tile_ids = slot_tile[0].reshape(-1)
-    backward = (lat_dev - 1 - tile_ids // tiles_lat) * tiles_lat + tile_ids % tiles_lat
-    tile_ids = jnp.where(band_index < peer_count // 2, tile_ids, backward)
+    tile_lat = tile_ids // tiles_lat
+    tile_lat = jnp.where(band_index < peer_count // 2, tile_lat, lat_dev - 1 - tile_lat)
+    tile_ids = tile_ids % tiles_lat * lat_dev + tile_lat
     onehot = (jnp.arange(tile_dev, dtype=jnp.int32)[:, None] == tile_ids[None, :]).astype(
         jnp.float32
     )
@@ -302,30 +382,8 @@
         precision=lax.Precision.HIGHEST,
         preferred_element_type=jnp.float32,
     )
-    lat_field = (
-        assembled.reshape(lat_dev, LONS // tile_width, field_rows, tile_width)
-        .transpose(2, 0, 1, 3)
-        .reshape(field_rows * lat_dev, LONS)
-    )
-    base_cos, base_sin, offset_cos, offset_sin = dft_base(wave_order, LONS, tile_width)
-    cosine = offset_cos[:, :, None] * base_cos[:, None, :] - offset_sin[:, :, None] * base_sin[:, None, :]
-    sine = offset_sin[:, :, None] * base_cos[:, None, :] + offset_cos[:, :, None] * base_sin[:, None, :]
-    table = jnp.concatenate(
-        [cosine.reshape(peer_count, wave_dev, LONS), -sine.reshape(peer_count, wave_dev, LONS)],
-        axis=1,
-    ).reshape(2 * WAVES, LONS)
-    fourier = lax.dot_general(
-        lat_field,
-        table,
-        (((1,), (1,)), ((), ())),
-        precision=lax.Precision.HIGH,
-        preferred_element_type=jnp.float32,
-    )
-    sent = (
-        fourier.reshape(field_rows, lat_dev, peer_count, 2 * wave_dev)
-        .transpose(2, 1, 0, 3)
-        .reshape(peer_count, lat_dev, 2 * field_rows * wave_dev)
-    )
+    tables = dft_base(wave_order, LONS, tile_width, peer_count)
+    sent = fourier_blocks(assembled, tables, peer_count, lat_dev, field_rows)
     local_waves = lax.dynamic_slice_in_dim(wave_order, band_index * wave_dev, wave_dev, 0)
     spectra, energy = legendre_project(local_waves, sent, WAVES, LATS)
     energy = energy[: field_rows // 2, : WAVES // peer_count]

time: 84.9 us -> 71.2 us (0.84)
  local copies, waits for them, and re-layouts: 16 us -> 5.7 us
  matrix products: 8.3 us -> 2.04 us
  Pallas kernels: 41 us -> 45.8 us
  other arithmetic: 11 us -> 9.05 us
    dot_general x1 -> x0, matrix products: 6.2 us -> none  [shards(): lax.dot_general(lat_field, table, (((1,), (1,)), ((), ())), precision=lax...]
    pallas_call x0 -> x1, Pallas kernels: none -> 4.84 us  [fourier_blocks(): pl.pallas_call(dft_kernel, grid=(table_rows // block,), out_shape=jax.Sha...]
    sub x1 -> x0, other arithmetic: 3.89 us -> none  [shards(): offset_cos[:, :, None] * base_cos[:, None, :]]
    transpose x1 -> x0, local copies, waits for them, and re-layouts: 2.97 us -> none  [shards(): sent = fourier.reshape(field_rows, lat_dev, peer_count, 2 * wave_dev).tra...]
    sub x1 -> x0, local copies, waits for them, and re-layouts: 2.72 us -> none  [shards(): offset_cos[:, :, None] * base_cos[:, None, :]]
    neg x1 -> x0, local copies, waits for them, and re-layouts: 2.7 us -> none  [shards(): -sine.reshape(peer_count, wave_dev, LONS)]
    reshape x1 -> x2, local copies, waits for them, and re-layouts: 1.93 us -> 0.16 us  [by_peer(): rows.reshape(peers, -1, rows.shape[-1])]
    concatenate x0 -> x3, other arithmetic: none -> 1.42 us  [by_peer(): return jnp.concatenate(both, axis=1).reshape(-1, real_rows.shape[-1])]
  transfers between devices with their start and end apart: 1 -> 1, of which waited for: 0 -> 0; matrix products, arithmetic and copies ran while one was open for 18% -> 13% of each run, Pallas kernels for 0% -> 0%
where the time goes in v4:
time: 71.2 us; the launch traced here: 70.8 us
  Pallas kernels  45.8 us (64%)
  other arithmetic  9.05 us (13%)
  starting transfers between devices  7.43 us (10%)
  local copies, waits for them, and re-layouts  5.7 us (8%)
  matrix products  2.04 us (3%)
  between operations  0.81 us (1%)
    pallas_call x1, Pallas kernels, legendre_project(): pl.pallas_call(project_kernel, out_shape=(jax.ShapeDtypeStruct((row_count...  41 us
    all_to_all x1, starting transfers between devices, shards(): lax.all_to_all(picked, 'band', split_axis=0, concat_axis=0, tiled=True)  7.43 us
    pallas_call x1, Pallas kernels, fourier_blocks(): pl.pallas_call(dft_kernel, grid=(table_rows // block,), out_shape=jax.Sha...  4.84 us
    mul x1, other arithmetic, dft_base(): jnp.sin(base) * norm_factor  2.57 us
    gather x1, local copies, waits for them, and re-layouts, shards(): picked = blocks[slot_block[0]]  1.56 us
    dot_general x1, matrix products, shards(): jnp.einsum('skfc,skcg->skfg', arrived, remap_tiles[0], preferred_element_...  1.46 us
  transfers between devices with their start and end apart: 1, of which 0 were waited for; matrix products, arithmetic and copies ran while one was open for 13% of the time, Pallas kernels for 0%

profile of v4, /device:TPU:0, one launch (start us, length us, event | category | flops | bytes accessed | tf_op | source)
XLA Modules:
  0.0 70.8 jit_solution(14317558988014444989)
XLA Ops:
  0.6 0.8 %compare_select_fusion = s32[16,3,1]{0,2,1:T(1,128)S(1)} fusion(s32[1,16,3]{1,0,2:T(1,128)} %param.7), kind=kLoop, calls=%fused_computation.35 | loop fusion | flops 144 | bytes 384 | tf_op jit(solution)/shard_map/select_n | solution.py:364
  1.5 0.1 reshape.378
  1.6 0.7 %iota_compare_fusion.2 = pred[16,3]{1,0:T(8,128)(4,1)S(1)} fusion(s32[16]{0:T(128)} %bitcast.43), kind=kLoop, calls=%fused_computation.38 | loop fusion | flops 48 | bytes 112 | tf_op jit(solution)/shard_map/lt | solution.py:365
  2.4 1.6 %gather_fusion = bf16[48,8,128]{2,1,0:T(8,128)(2,1)S(1)} fusion(bf16[128,8,128]{2,1,0:T(8,128)(2,1)} %bitcast.42, s32[1024]{0:T(1024)S(1)} %pad_clamp_fusion), kind=kCustom, calls=%fused_computation | custom fusion | bytes 196800 | tf_op jit(solution)/shard_map/gather | solution.py:364
  3.9 0.8 %broadcast_select_fusion = bf16[16,3,8,128]{3,2,1,0:T(8,128)(2,1)} fusion(bf16[16,3,8,128]{3,2,1,0:T(8,128)(2,1)S(1)} %bitcast.41, pred[16,3]{1,0:T(8,128)(4,1)S(1)} %iota_compare_fusion.2), kind=kLoop, calls=%fused_computation.20 | loop fusion | flops 49152 | bytes 196656 | tf_op jit(solution)/shard_map/jit(_where)/select_n | solution.py:366
  4.7 7.4 %all-to-all-start = ((bf16[16,3,8,128]{3,2,1,0:T(8,128)(2,1)}), bf16[16,3,8,128]{3,2,1,0:T(8,128)(2,1)}, u32[]{:S(2)}, u32[]{:S(2)}) async-start(bf16[16,3,8,128]{3,2,1,0:T(8,128)(2,1)} %broadcast_select_fusion), calls=%async_computation | async-start | bytes 196608 | tf_op jit(solution)/shard_map/all_to_all | solution.py:367
  12.2 2.6 %sine_multiply_fusion = (f32[512,128]{1,0:T(8,128)S(1)}, f32[512,128]{1,0:T(8,128)}) fusion(s32[512]{0:T(512)} %param.11), kind=kLoop, calls=%fused_computation.11 | loop fusion | flops 1048576 | bytes 526336 | tf_op jit(solution)/shard_map/mul | solution.py:34
  14.8 0.8 %add_multiply_fusion.1 = (f32[32]{0:T(128)S(1)}, f32[32]{0:T(128)S(1)}) fusion(s32[512]{0:T(512)} %param.11, s32[]{:T(128)S(6)} %select_n.61), kind=kLoop, calls=%fused_computation.91 | loop fusion | flops 3520 | bytes 388 | tf_op jit(solution)/shard_map/mul | solution.py:303
  15.6 0.8 %dynamic-slice_bitcast_fusion = s32[32,1]{0,1:T(1,128)S(1)} fusion(s32[512]{0:T(512)} %param.11, s32[]{:T(128)S(6)} %select_n.61), kind=kLoop, calls=%fused_computation.95 | loop fusion | bytes 260 | tf_op jit(solution)/shard_map/broadcast_in_dim | solution.py:340
  16.5 0.8 %fusion.15 = (f32[512,8]{0,1:T(8,128)S(1)}, f32[512,8]{0,1:T(8,128)S(1)}) fusion(s32[8]{0:T(128)S(1)} %iota_multiply_fusion.1, s32[512]{0:T(512)} %param.11), kind=kLoop, calls=%fused_computation.36 | loop fusion | flops 57344 | bytes 34848 | tf_op jit(solution)/shard_map/sin | solution.py:34
  17.3 0.7 %neg.3 = f32[512,128]{1,0:T(8,128)} negate(f32[512,128]{1,0:T(8,128)S(1)} %get-tuple-element.9) | non-fusion elementwise | flops 65536 | bytes 524288 | tf_op jit(solution)/shard_map/neg | solution.py:42
  18.2 0.2 copy.30
  18.5 0.1 pad_maximum_fusion.3
  18.6 1.0 %copy.31 = f32[16,64,8]{2,1,0:T(8,128)} copy(f32[16,64,8]{1,0,2:T(8,128)S(1)} %pad_maximum_fusion.3) | data formatting | bytes 65536 | tf_op jit(solution)/shard_map/concatenate | solution.py:39
  19.7 0.1 reshape_squeeze.3
  19.8 0.1 copy.32.order_ref
  20.0 1.2 %pad_maximum_fusion.1 = (f32[16,64,128]{2,1,0:T(8,128)S(1)}, f32[16,64,128]{2,1,0:T(8,128)S(1)}) fusion(f32[16,32,128]{2,1,0:T(8,128)} %bitcast.38, f32[16,32,128]{2,1,0:T(8,128)S(1)} %bitcast.37, f32[16,32,128]{2,1,0:T(8,128)} %bitcast.39), kind=kLoop, calls=%fused_computation.4 | loop fusion | flops 262144 | bytes 1835008 | tf_op jit(solution)/shard_map/concatenate | solution.py:39
  21.2 0.1 divide_sqrt_fusion
  21.4 1.5 %fusion = f32[16,3,8,128]{3,2,1,0:T(8,128)S(1)} fusion(bf16[16,3,8,128]{3,2,1,0:T(8,128)(2,1)} %all-to-all-done, bf16[1,16,3,128,128]{4,3,2,1,0:T(8,128)(2,1)S(1)} %copy-done), kind=kOutput, calls=%fused_computation.1 | convolution fusion | flops 12582912 | bytes 1867776 | tf_op jit(solution)/shard_map/skfc,skcg->skfg/dot_general | solution.py:368
  22.9 0.6 fusion.8.field_ref
  23.5 4.8 %fourier.1.sent_ref = f32[16,32,512]{2,1,0:T(8,128)S(1)} custom-call(f32[256,1024]{1,0:T(8,128)S(1)} %fusion.8.field_ref, f32[1024,128]{1,0:T(8,128)S(1)} %bitcast.33, f32[1024,128]{1,0:T(8,128)S(1)} %bitcast.32, f32[1024,8]{1,0:T(8,128)S(1)} %bitcast.34, f32[1024,8]{1,0:T(8,128)S(1)} %bitcast.35), custom_call_target="tpu_custom_call" | custom-call | tf_op jit(solution)/shard_map/fourier/pallas_call | solution.py:112
  28.3 41.0 %project.1 = (f32[32,16,512]{2,1,0:T(8,128)S(1)}, f32[8,128]{1,0:T(8,128)S(1)}) custom-call(s32[32,1]{1,0:T(8,128)S(1)} %copy.32.order_ref, f32[32,512]{1,0:T(8,128)S(1)} %get-tuple-element.23.first_ref, f32[32,512]{1,0:T(8,128)S(1)} %get-tuple-element.22.second_ref, f32[32,256]{1,0:T(8,128)S(1)} %multiply_add_fusion.start_ref, ...), custom_call_target="tpu_custom_call" | custom-call | tf_op jit(solution)/shard_map/project/pallas_call | solution.py:319
  69.3 0.6 slice.3
  69.9 1.0 %copy.39 = f32[32,2,8,512]{3,2,1,0:T(8,128)} copy(f32[32,2,8,512]{3,2,1,0:T(8,128)S(1)} %bitcast.36) | data formatting | bytes 2097152
  (22 shorter events, 0.7 us)
Async XLA Ops:
  0.6 20.8 %copy-start = (bf16[1,16,3,128,128]{4,3,2,1,0:T(8,128)(2,1)S(1)}, bf16[1,16,3,128,128]{4,3,2,1,0:T(8,128)(2,1)}, u32[]{:S(2)}) copy-start(bf16[1,16,3,128,128]{4,3,2,1,0:T(8,128)(2,1)} %param.10) | copy-start | bytes 4718596
  3.9 15.7 %copy-start.2 = (s32[1,16,3]{1,0,2:T(1,128)S(1)}, s32[1,16,3]{1,0,2:T(1,128)}, u32[]{:S(2)}) copy-start(s32[1,16,3]{1,0,2:T(1,128)} %param.9) | copy-start | bytes 580
  4.7 16.7 %all-to-all-start = ((bf16[16,3,8,128]{3,2,1,0:T(8,128)(2,1)}), bf16[16,3,8,128]{3,2,1,0:T(8,128)(2,1)}, u32[]{:S(2)}, u32[]{:S(2)}) async-start(bf16[16,3,8,128]{3,2,1,0:T(8,128)(2,1)} %broadcast_select_fusion), calls=%async_computation | async-start | bytes 196608 | tf_op jit(solution)/shard_map/all_to_all | solution.py:367
  21.4 2.1 %copy-start.1 = (f32[16,64,8]{2,1,0:T(8,128)S(1)}, f32[16,64,8]{2,1,0:T(8,128)}, u32[]{:S(2)}) copy-start(f32[16,64,8]{2,1,0:T(8,128)} %copy.31) | copy-start | bytes 98308

commit v5 on v4

--- a/solution.py
+++ b/solution.py
@@ -13,6 +13,9 @@
 DEG_BLOCK = 128
 STEPS = 8
 ROW_GAP = 8
+SIDE = 128
+TOP_CODE = 32600.0
+CODE_STEP = math.log(2.0) / 256.0
 
 
 def gauss_half(lat_count):
@@ -59,7 +62,7 @@
 
 
 def dft_kernel(field_ref, base_c_ref, base_s_ref, offset_c_ref, offset_s_ref, sent_ref):
-    dests, lat_dev, width = sent_ref.shape
+    dests, lat_dev, _ = sent_ref.shape
     rows, points = base_c_ref.shape
     tiles = offset_c_ref.shape[1]
     fields = field_ref.shape[1] // points
@@ -91,13 +94,19 @@
         with_high = dot_nt(jnp.concatenate([field_high, field_low], axis=0), table_high)
         total = total + (with_high[:height] + with_high[height:] + dot_nt(field_high, table_low))
     for dest in range(dests):
-        sent_ref[dest] = jnp.concatenate(
+        values = jnp.concatenate(
             [
                 total[row * lat_dev : (row + 1) * lat_dev, dest * per_dest : (dest + 1) * per_dest]
                 for row in range(fields)
             ],
             axis=1,
         )
+        peak = jnp.maximum(jnp.max(jnp.abs(values), axis=1, keepdims=True), 1e-30)
+        code = jnp.ceil(jnp.log(peak) * (1.0 / CODE_STEP))
+        steps = jnp.floor(values * (jnp.exp(-code * CODE_STEP) * TOP_CODE) + 0.5)
+        side = jnp.broadcast_to(code, (lat_dev, SIDE))
+        coded = jnp.concatenate([steps, side], axis=1)
+        sent_ref[dest] = coded.astype(jnp.int32).astype(jnp.int16)
 
 
 def fourier_blocks(field, tables, peers, lat_dev, fields):
@@ -106,13 +115,13 @@
     block = 256
     per_dest = table_rows // peers
     dests = block // per_dest
-    width = fields * per_dest
+    width = fields * per_dest + SIDE
     row_block = pl.BlockSpec((block, points), lambda step: (step, 0))
     offset_block = pl.BlockSpec((block, tiles), lambda step: (step, 0))
     return pl.pallas_call(
         dft_kernel,
         grid=(table_rows // block,),
-        out_shape=jax.ShapeDtypeStruct((peers, lat_dev, width), jnp.float32),
+        out_shape=jax.ShapeDtypeStruct((peers, lat_dev, width), jnp.int16),
         in_specs=[
             pl.BlockSpec(field.shape, lambda step: (0, 0)),
             row_block,
@@ -152,6 +161,7 @@
     energy_recv_sem,
 ):
     peers, lat_dev, width = sent_ref.shape
+    width = width - SIDE
     rows = order_ref.shape[0]
     half = mu_ref.shape[1]
     total_n = first_ref.shape[1]
@@ -168,13 +178,12 @@
     pl.semaphore_wait(barrier, peers - 1)
 
     place_me = me + (me // (peers // 2)) * (peers // 2 + peers - 1 - 2 * me)
-    landing = pl.ds(pl.multiple_of(place_me * lat_dev, lat_dev), lat_dev)
     copies = []
     for hop in range(1, peers):
         peer = lax.rem(me + hop, peers)
         copy = pltpu.make_async_remote_copy(
             src_ref=sent_ref.at[peer],
-            dst_ref=landed.at[landing, :],
+            dst_ref=landed.at[place_me],
             send_sem=send_sem.at[hop],
             recv_sem=recv_sem.at[hop],
             device_id={"band": peer},
@@ -182,7 +191,7 @@
         )
         copy.start()
         copies.append(copy)
-    landed[landing, :] = sent_ref[me]
+    landed[place_me] = sent_ref[me]
 
     order_wide = jnp.broadcast_to(order_ref[...], (rows, half))
     mu_row = jnp.broadcast_to(mu_ref[...], (8, half))
@@ -223,10 +232,18 @@
         copy.wait()
 
     lat_scale = lat_scale_ref[...]
+
+    def load_half(first_peer, span):
+        coded = landed[pl.ds(first_peer, peers // 2), :, span]
+        return coded.astype(jnp.int32).astype(jnp.float32).reshape(half, 128)
+
+    side = pl.ds(width, SIDE)
+    north_scale = jnp.exp(load_half(0, side) * CODE_STEP) * (1.0 / TOP_CODE)
+    south_scale = jnp.exp(load_half(peers // 2, side) * CODE_STEP) * (1.0 / TOP_CODE)
     for group in range(width // 128):
         span = pl.ds(group * 128, 128)
-        north = landed[pl.ds(0, half), span]
-        south = landed[pl.ds(half, half), span]
+        north = load_half(0, span) * north_scale
+        south = load_half(peers // 2, span) * south_scale
         even = (north + south).T * lat_scale
         odd = (north - south).T * lat_scale
         even_left[span, :] = even[:, : half // 2]
@@ -293,6 +310,7 @@
 
 def legendre_project(wave_vals, sent, total_n, lat_count):
     peers, lat_dev, width = sent.shape
+    width = width - SIDE
     row_count = wave_vals.shape[0]
     col_count = width // row_count
     half_lat = lat_count // 2
@@ -325,7 +343,7 @@
         in_specs=[pl.BlockSpec(memory_space=pltpu.VMEM)] * 8,
         out_specs=[pl.BlockSpec(memory_space=pltpu.VMEM)] * 2,
         scratch_shapes=[pltpu.VMEM((row_count * (total_n + ROW_GAP), half_lat // 2), jnp.float32)] * 2
-        + [pltpu.VMEM((lat_count, width), jnp.float32)]
+        + [pltpu.VMEM((peers, lat_dev, width + SIDE), jnp.int16)]
         + [pltpu.VMEM((width, half_lat // 2), jnp.float32)] * 4
         + [
             pltpu.VMEM((total_n // 128, 8, 128), jnp.float32),

time: 71.2 us -> 63.9 us (0.90)
  Pallas kernels: 45.8 us -> 38.5 us
    pallas_call x1, Pallas kernels: 41 us -> 33 us  [legendre_project(): pl.pallas_call(project_kernel, out_shape=(jax.ShapeDtypeStruct((row_count...]
  transfers between devices with their start and end apart: 1 -> 1, of which waited for: 0 -> 0; matrix products, arithmetic and copies ran while one was open for 13% -> 14% of each run, Pallas kernels for 0% -> 0%
where the time goes in v5:
time: 63.9 us; the launch traced here: 63.5 us
  Pallas kernels  38.5 us (60%)
  other arithmetic  9.05 us (14%)
  starting transfers between devices  7.43 us (12%)
  local copies, waits for them, and re-layouts  5.7 us (9%)
  matrix products  2.04 us (3%)
  between operations  0.81 us (1%)
    pallas_call x1, Pallas kernels, legendre_project(): pl.pallas_call(project_kernel, out_shape=(jax.ShapeDtypeStruct((row_count...  33 us
    all_to_all x1, starting transfers between devices, shards(): lax.all_to_all(picked, 'band', split_axis=0, concat_axis=0, tiled=True)  7.43 us
    pallas_call x1, Pallas kernels, fourier_blocks(): pl.pallas_call(dft_kernel, grid=(table_rows // block,), out_shape=jax.Sha...  5.52 us
    mul x1, other arithmetic, dft_base(): jnp.sin(base) * norm_factor  2.57 us
    gather x1, local copies, waits for them, and re-layouts, shards(): picked = blocks[slot_block[0]]  1.56 us
    dot_general x1, matrix products, shards(): jnp.einsum('skfc,skcg->skfg', arrived, remap_tiles[0], preferred_element_...  1.46 us
    concatenate x3, other arithmetic, by_peer(): return jnp.concatenate(both, axis=1).reshape(-1, real_rows.shape[-1])  1.42 us
  transfers between devices with their start and end apart: 1, of which 0 were waited for; matrix products, arithmetic and copies ran while one was open for 14% of the time, Pallas kernels for 0%

profile of v5, /device:TPU:0, one launch (start us, length us, event | category | flops | bytes accessed | tf_op | source)
XLA Modules:
  0.0 63.5 jit_solution(5724522076691782783)
XLA Ops:
  0.6 0.8 %compare_select_fusion = s32[16,3,1]{0,2,1:T(1,128)S(1)} fusion(s32[1,16,3]{1,0,2:T(1,128)} %param.7), kind=kLoop, calls=%fused_computation.35 | loop fusion | flops 144 | bytes 384 | tf_op jit(solution)/shard_map/select_n | solution.py:382
  1.5 0.1 reshape.378
  1.6 0.7 %iota_compare_fusion.2 = pred[16,3]{1,0:T(8,128)(4,1)S(1)} fusion(s32[16]{0:T(128)} %bitcast.43), kind=kLoop, calls=%fused_computation.38 | loop fusion | flops 48 | bytes 112 | tf_op jit(solution)/shard_map/lt | solution.py:383
  2.4 1.6 %gather_fusion = bf16[48,8,128]{2,1,0:T(8,128)(2,1)S(1)} fusion(bf16[128,8,128]{2,1,0:T(8,128)(2,1)} %bitcast.42, s32[1024]{0:T(1024)S(1)} %pad_clamp_fusion), kind=kCustom, calls=%fused_computation | custom fusion | bytes 196800 | tf_op jit(solution)/shard_map/gather | solution.py:382
  3.9 0.8 %broadcast_select_fusion = bf16[16,3,8,128]{3,2,1,0:T(8,128)(2,1)} fusion(bf16[16,3,8,128]{3,2,1,0:T(8,128)(2,1)S(1)} %bitcast.41, pred[16,3]{1,0:T(8,128)(4,1)S(1)} %iota_compare_fusion.2), kind=kLoop, calls=%fused_computation.20 | loop fusion | flops 49152 | bytes 196656 | tf_op jit(solution)/shard_map/jit(_where)/select_n | solution.py:384
  4.7 7.4 %all-to-all-start = ((bf16[16,3,8,128]{3,2,1,0:T(8,128)(2,1)}), bf16[16,3,8,128]{3,2,1,0:T(8,128)(2,1)}, u32[]{:S(2)}, u32[]{:S(2)}) async-start(bf16[16,3,8,128]{3,2,1,0:T(8,128)(2,1)} %broadcast_select_fusion), calls=%async_computation | async-start | bytes 196608 | tf_op jit(solution)/shard_map/all_to_all | solution.py:385
  12.2 2.6 %sine_multiply_fusion = (f32[512,128]{1,0:T(8,128)S(1)}, f32[512,128]{1,0:T(8,128)}) fusion(s32[512]{0:T(512)} %param.11), kind=kLoop, calls=%fused_computation.11 | loop fusion | flops 1048576 | bytes 526336 | tf_op jit(solution)/shard_map/mul | solution.py:37
  14.8 0.8 %add_multiply_fusion.1 = (f32[32]{0:T(128)S(1)}, f32[32]{0:T(128)S(1)}) fusion(s32[512]{0:T(512)} %param.11, s32[]{:T(128)S(6)} %select_n.61), kind=kLoop, calls=%fused_computation.91 | loop fusion | flops 3520 | bytes 388 | tf_op jit(solution)/shard_map/mul | solution.py:321
  15.6 0.8 %dynamic-slice_bitcast_fusion = s32[32,1]{0,1:T(1,128)S(1)} fusion(s32[512]{0:T(512)} %param.11, s32[]{:T(128)S(6)} %select_n.61), kind=kLoop, calls=%fused_computation.95 | loop fusion | bytes 260 | tf_op jit(solution)/shard_map/broadcast_in_dim | solution.py:358
  16.5 0.8 %fusion.15 = (f32[512,8]{0,1:T(8,128)S(1)}, f32[512,8]{0,1:T(8,128)S(1)}) fusion(s32[8]{0:T(128)S(1)} %iota_multiply_fusion.1, s32[512]{0:T(512)} %param.11), kind=kLoop, calls=%fused_computation.36 | loop fusion | flops 57344 | bytes 34848 | tf_op jit(solution)/shard_map/sin | solution.py:37
  17.3 0.7 %neg.3 = f32[512,128]{1,0:T(8,128)} negate(f32[512,128]{1,0:T(8,128)S(1)} %get-tuple-element.9) | non-fusion elementwise | flops 65536 | bytes 524288 | tf_op jit(solution)/shard_map/neg | solution.py:45
  18.2 0.2 copy.30
  18.5 0.1 pad_maximum_fusion.3
  18.6 1.0 %copy.31 = f32[16,64,8]{2,1,0:T(8,128)} copy(f32[16,64,8]{1,0,2:T(8,128)S(1)} %pad_maximum_fusion.3) | data formatting | bytes 65536 | tf_op jit(solution)/shard_map/concatenate | solution.py:42
  19.7 0.1 reshape_squeeze.3
  19.8 0.1 copy.32.order_ref
  20.0 1.2 %pad_maximum_fusion.1 = (f32[16,64,128]{2,1,0:T(8,128)S(1)}, f32[16,64,128]{2,1,0:T(8,128)S(1)}) fusion(f32[16,32,128]{2,1,0:T(8,128)} %bitcast.38, f32[16,32,128]{2,1,0:T(8,128)S(1)} %bitcast.37, f32[16,32,128]{2,1,0:T(8,128)} %bitcast.39), kind=kLoop, calls=%fused_computation.4 | loop fusion | flops 262144 | bytes 1835008 | tf_op jit(solution)/shard_map/concatenate | solution.py:42
  21.2 0.1 divide_sqrt_fusion
  21.4 1.5 %fusion = f32[16,3,8,128]{3,2,1,0:T(8,128)S(1)} fusion(bf16[16,3,8,128]{3,2,1,0:T(8,128)(2,1)} %all-to-all-done, bf16[1,16,3,128,128]{4,3,2,1,0:T(8,128)(2,1)S(1)} %copy-done), kind=kOutput, calls=%fused_computation.1 | convolution fusion | flops 12582912 | bytes 1867776 | tf_op jit(solution)/shard_map/skfc,skcg->skfg/dot_general | solution.py:386
  22.9 0.6 fusion.8.field_ref
  23.5 5.5 %fourier.1.sent_ref = s16[16,32,640]{2,1,0:T(8,128)(2,1)S(1)} custom-call(f32[256,1024]{1,0:T(8,128)S(1)} %fusion.8.field_ref, f32[1024,128]{1,0:T(8,128)S(1)} %bitcast.33, f32[1024,128]{1,0:T(8,128)S(1)} %bitcast.32, f32[1024,8]{1,0:T(8,128)S(1)} %bitcast.34, f32[1024,8]{1,0:T(8,128)S(1)} %bitcast.35), custom_call_target="tpu_custom_call" | custom-call | tf_op jit(solution)/shard_map/fourier/pallas_call | solution.py:121
  29.0 33.0 %project.1 = (f32[32,16,512]{2,1,0:T(8,128)S(1)}, f32[8,128]{1,0:T(8,128)S(1)}) custom-call(s32[32,1]{1,0:T(8,128)S(1)} %copy.32.order_ref, f32[32,512]{1,0:T(8,128)S(1)} %get-tuple-element.23.first_ref, f32[32,512]{1,0:T(8,128)S(1)} %get-tuple-element.22.second_ref, f32[32,256]{1,0:T(8,128)S(1)} %multiply_add_fusion.start_ref, ...), custom_call_target="tpu_custom_call" | custom-call | tf_op jit(solution)/shard_map/project/pallas_call | solution.py:337
  62.0 0.6 slice.3
  62.6 1.0 %copy.39 = f32[32,2,8,512]{3,2,1,0:T(8,128)} copy(f32[32,2,8,512]{3,2,1,0:T(8,128)S(1)} %bitcast.36) | data formatting | bytes 2097152
  (22 shorter events, 0.7 us)
Async XLA Ops:
  0.6 20.8 %copy-start = (bf16[1,16,3,128,128]{4,3,2,1,0:T(8,128)(2,1)S(1)}, bf16[1,16,3,128,128]{4,3,2,1,0:T(8,128)(2,1)}, u32[]{:S(2)}) copy-start(bf16[1,16,3,128,128]{4,3,2,1,0:T(8,128)(2,1)} %param.10) | copy-start | bytes 4718596
  3.9 15.7 %copy-start.2 = (s32[1,16,3]{1,0,2:T(1,128)S(1)}, s32[1,16,3]{1,0,2:T(1,128)}, u32[]{:S(2)}) copy-start(s32[1,16,3]{1,0,2:T(1,128)} %param.9) | copy-start | bytes 580
  4.7 16.7 %all-to-all-start = ((bf16[16,3,8,128]{3,2,1,0:T(8,128)(2,1)}), bf16[16,3,8,128]{3,2,1,0:T(8,128)(2,1)}, u32[]{:S(2)}, u32[]{:S(2)}) async-start(bf16[16,3,8,128]{3,2,1,0:T(8,128)(2,1)} %broadcast_select_fusion), calls=%async_computation | async-start | bytes 196608 | tf_op jit(solution)/shard_map/all_to_all | solution.py:385
  21.4 2.1 %copy-start.1 = (f32[16,64,8]{2,1,0:T(8,128)S(1)}, f32[16,64,8]{2,1,0:T(8,128)}, u32[]{:S(2)}) copy-start(f32[16,64,8]{2,1,0:T(8,128)} %copy.31) | copy-start | bytes 98308

commit v6 on v5

--- a/solution.py
+++ b/solution.py
@@ -280,7 +280,7 @@
         return total + (squares[:fields] + squares[fields:]) * weight
 
     total = lax.fori_loop(
-        0, rows, wave_step, jnp.zeros((fields, total_n), jnp.float32), unroll=2
+        0, rows, wave_step, jnp.zeros((fields, total_n), jnp.float32), unroll=4
     )
     total = (total + pltpu.roll(total, fields // 2, 0)) * degree_scale_ref[...]
     for group in range(total_n // 128):
@@ -397,7 +397,7 @@
     assembled = jnp.dot(
         onehot,
         contribs.reshape(-1, field_rows * tile_width),
-        precision=lax.Precision.HIGHEST,
+        precision=lax.Precision.HIGH,
         preferred_element_type=jnp.float32,
     )
     tables = dft_base(wave_order, LONS, tile_width, peer_count)

time: 63.9 us -> 62.9 us (0.984)
  Pallas kernels: 38.5 us -> 37.6 us
    pallas_call x1, Pallas kernels: 33 us -> 32.1 us  [legendre_project(): pl.pallas_call(project_kernel, out_shape=(jax.ShapeDtypeStruct((row_count...]
  transfers between devices with their start and end apart: 1 -> 1, of which waited for: 0 -> 0; matrix products, arithmetic and copies ran while one was open for 14% -> 15% of each run, Pallas kernels for 0% -> 0%
where the time goes in v6:
time: 62.9 us; the launch traced here: 62.5 us
  Pallas kernels  37.6 us (60%)
  other arithmetic  9.05 us (14%)
  starting transfers between devices  7.43 us (12%)
  local copies, waits for them, and re-layouts  5.7 us (9%)
  matrix products  1.9 us (3%)
  between operations  0.81 us (1%)
    pallas_call x1, Pallas kernels, legendre_project(): pl.pallas_call(project_kernel, out_shape=(jax.ShapeDtypeStruct((row_count...  32.1 us
    all_to_all x1, starting transfers between devices, shards(): lax.all_to_all(picked, 'band', split_axis=0, concat_axis=0, tiled=True)  7.43 us
    pallas_call x1, Pallas kernels, fourier_blocks(): pl.pallas_call(dft_kernel, grid=(table_rows // block,), out_shape=jax.Sha...  5.54 us
    mul x1, other arithmetic, dft_base(): jnp.sin(base) * norm_factor  2.57 us
    gather x1, local copies, waits for them, and re-layouts, shards(): picked = blocks[slot_block[0]]  1.56 us
    dot_general x1, matrix products, shards(): jnp.einsum('skfc,skcg->skfg', arrived, remap_tiles[0], preferred_element_...  1.46 us
    concatenate x3, other arithmetic, by_peer(): return jnp.concatenate(both, axis=1).reshape(-1, real_rows.shape[-1])  1.42 us
  transfers between devices with their start and end apart: 1, of which 0 were waited for; matrix products, arithmetic and copies ran while one was open for 15% of the time, Pallas kernels for 0%

profile of v6, /device:TPU:0, one launch (start us, length us, event | category | flops | bytes accessed | tf_op | source)
XLA Modules:
  0.0 62.5 jit_solution(10283673343282028428)
XLA Ops:
  0.6 0.8 %compare_select_fusion = s32[16,3,1]{0,2,1:T(1,128)S(1)} fusion(s32[1,16,3]{1,0,2:T(1,128)} %param.7), kind=kLoop, calls=%fused_computation.35 | loop fusion | flops 144 | bytes 384 | tf_op jit(solution)/shard_map/select_n | solution.py:382
  1.5 0.1 reshape.378
  1.6 0.7 %iota_compare_fusion.2 = pred[16,3]{1,0:T(8,128)(4,1)S(1)} fusion(s32[16]{0:T(128)} %bitcast.43), kind=kLoop, calls=%fused_computation.38 | loop fusion | flops 48 | bytes 112 | tf_op jit(solution)/shard_map/lt | solution.py:383
  2.4 1.6 %gather_fusion = bf16[48,8,128]{2,1,0:T(8,128)(2,1)S(1)} fusion(bf16[128,8,128]{2,1,0:T(8,128)(2,1)} %bitcast.42, s32[1024]{0:T(1024)S(1)} %pad_clamp_fusion), kind=kCustom, calls=%fused_computation | custom fusion | bytes 196800 | tf_op jit(solution)/shard_map/gather | solution.py:382
  3.9 0.8 %broadcast_select_fusion = bf16[16,3,8,128]{3,2,1,0:T(8,128)(2,1)} fusion(bf16[16,3,8,128]{3,2,1,0:T(8,128)(2,1)S(1)} %bitcast.41, pred[16,3]{1,0:T(8,128)(4,1)S(1)} %iota_compare_fusion.2), kind=kLoop, calls=%fused_computation.20 | loop fusion | flops 49152 | bytes 196656 | tf_op jit(solution)/shard_map/jit(_where)/select_n | solution.py:384
  4.7 7.4 %all-to-all-start = ((bf16[16,3,8,128]{3,2,1,0:T(8,128)(2,1)}), bf16[16,3,8,128]{3,2,1,0:T(8,128)(2,1)}, u32[]{:S(2)}, u32[]{:S(2)}) async-start(bf16[16,3,8,128]{3,2,1,0:T(8,128)(2,1)} %broadcast_select_fusion), calls=%async_computation | async-start | bytes 196608 | tf_op jit(solution)/shard_map/all_to_all | solution.py:385
  12.2 2.6 %sine_multiply_fusion = (f32[512,128]{1,0:T(8,128)S(1)}, f32[512,128]{1,0:T(8,128)}) fusion(s32[512]{0:T(512)} %param.11), kind=kLoop, calls=%fused_computation.11 | loop fusion | flops 1048576 | bytes 526336 | tf_op jit(solution)/shard_map/mul | solution.py:37
  14.8 0.8 %add_multiply_fusion.1 = (f32[32]{0:T(128)S(1)}, f32[32]{0:T(128)S(1)}) fusion(s32[512]{0:T(512)} %param.11, s32[]{:T(128)S(6)} %select_n.61), kind=kLoop, calls=%fused_computation.91 | loop fusion | flops 3520 | bytes 388 | tf_op jit(solution)/shard_map/mul | solution.py:321
  15.6 0.8 %dynamic-slice_bitcast_fusion = s32[32,1]{0,1:T(1,128)S(1)} fusion(s32[512]{0:T(512)} %param.11, s32[]{:T(128)S(6)} %select_n.61), kind=kLoop, calls=%fused_computation.95 | loop fusion | bytes 260 | tf_op jit(solution)/shard_map/broadcast_in_dim | solution.py:358
  16.5 0.8 %fusion.15 = (f32[512,8]{0,1:T(8,128)S(1)}, f32[512,8]{0,1:T(8,128)S(1)}) fusion(s32[8]{0:T(128)S(1)} %iota_multiply_fusion.1, s32[512]{0:T(512)} %param.11), kind=kLoop, calls=%fused_computation.36 | loop fusion | flops 57344 | bytes 34848 | tf_op jit(solution)/shard_map/sin | solution.py:37
  17.3 0.7 %neg.3 = f32[512,128]{1,0:T(8,128)} negate(f32[512,128]{1,0:T(8,128)S(1)} %get-tuple-element.9) | non-fusion elementwise | flops 65536 | bytes 524288 | tf_op jit(solution)/shard_map/neg | solution.py:45
  18.2 0.2 copy.30
  18.5 0.1 pad_maximum_fusion.3
  18.6 1.0 %copy.31 = f32[16,64,8]{2,1,0:T(8,128)} copy(f32[16,64,8]{1,0,2:T(8,128)S(1)} %pad_maximum_fusion.3) | data formatting | bytes 65536 | tf_op jit(solution)/shard_map/concatenate | solution.py:42
  19.7 0.1 reshape_squeeze.3
  19.8 0.1 copy.32.order_ref
  20.0 1.2 %pad_maximum_fusion.1 = (f32[16,64,128]{2,1,0:T(8,128)S(1)}, f32[16,64,128]{2,1,0:T(8,128)S(1)}) fusion(f32[16,32,128]{2,1,0:T(8,128)} %bitcast.38, f32[16,32,128]{2,1,0:T(8,128)S(1)} %bitcast.37, f32[16,32,128]{2,1,0:T(8,128)} %bitcast.39), kind=kLoop, calls=%fused_computation.4 | loop fusion | flops 262144 | bytes 1835008 | tf_op jit(solution)/shard_map/concatenate | solution.py:42
  21.2 0.1 divide_sqrt_fusion
  21.4 1.5 %fusion = f32[16,3,8,128]{3,2,1,0:T(8,128)S(1)} fusion(bf16[16,3,8,128]{3,2,1,0:T(8,128)(2,1)} %all-to-all-done, bf16[1,16,3,128,128]{4,3,2,1,0:T(8,128)(2,1)S(1)} %copy-done), kind=kOutput, calls=%fused_computation.1 | convolution fusion | flops 12582912 | bytes 1867776 | tf_op jit(solution)/shard_map/skfc,skcg->skfg/dot_general | solution.py:386
  22.9 0.4 fusion.8.field_ref
  23.3 5.5 %fourier.1.sent_ref = s16[16,32,640]{2,1,0:T(8,128)(2,1)S(1)} custom-call(f32[256,1024]{1,0:T(8,128)S(1)} %fusion.8.field_ref, f32[1024,128]{1,0:T(8,128)S(1)} %bitcast.33, f32[1024,128]{1,0:T(8,128)S(1)} %bitcast.32, f32[1024,8]{1,0:T(8,128)S(1)} %bitcast.34, f32[1024,8]{1,0:T(8,128)S(1)} %bitcast.35), custom_call_target="tpu_custom_call" | custom-call | tf_op jit(solution)/shard_map/fourier/pallas_call | solution.py:121
  28.9 32.1 %project.1 = (f32[32,16,512]{2,1,0:T(8,128)S(1)}, f32[8,128]{1,0:T(8,128)S(1)}) custom-call(s32[32,1]{1,0:T(8,128)S(1)} %copy.32.order_ref, f32[32,512]{1,0:T(8,128)S(1)} %get-tuple-element.23.first_ref, f32[32,512]{1,0:T(8,128)S(1)} %get-tuple-element.22.second_ref, f32[32,256]{1,0:T(8,128)S(1)} %multiply_add_fusion.start_ref, ...), custom_call_target="tpu_custom_call" | custom-call | tf_op jit(solution)/shard_map/project/pallas_call | solution.py:337
  60.9 0.6 slice.3
  61.5 1.0 %copy.39 = f32[32,2,8,512]{3,2,1,0:T(8,128)} copy(f32[32,2,8,512]{3,2,1,0:T(8,128)S(1)} %bitcast.36) | data formatting | bytes 2097152
  (22 shorter events, 0.7 us)
Async XLA Ops:
  0.6 20.8 %copy-start = (bf16[1,16,3,128,128]{4,3,2,1,0:T(8,128)(2,1)S(1)}, bf16[1,16,3,128,128]{4,3,2,1,0:T(8,128)(2,1)}, u32[]{:S(2)}) copy-start(bf16[1,16,3,128,128]{4,3,2,1,0:T(8,128)(2,1)} %param.10) | copy-start | bytes 4718596
  3.9 15.7 %copy-start.2 = (s32[1,16,3]{1,0,2:T(1,128)S(1)}, s32[1,16,3]{1,0,2:T(1,128)}, u32[]{:S(2)}) copy-start(s32[1,16,3]{1,0,2:T(1,128)} %param.9) | copy-start | bytes 580
  4.7 16.7 %all-to-all-start = ((bf16[16,3,8,128]{3,2,1,0:T(8,128)(2,1)}), bf16[16,3,8,128]{3,2,1,0:T(8,128)(2,1)}, u32[]{:S(2)}, u32[]{:S(2)}) async-start(bf16[16,3,8,128]{3,2,1,0:T(8,128)(2,1)} %broadcast_select_fusion), calls=%async_computation | async-start | bytes 196608 | tf_op jit(solution)/shard_map/all_to_all | solution.py:385
  21.4 1.9 %copy-start.1 = (f32[16,64,8]{2,1,0:T(8,128)S(1)}, f32[16,64,8]{2,1,0:T(8,128)}, u32[]{:S(2)}) copy-start(f32[16,64,8]{2,1,0:T(8,128)} %copy.31) | copy-start | bytes 98308
